TPU v7x, 32 devices: a whole 2x2x4 slice. The times are simulated.
32 devices in a mesh: dp: 4 (over y, x), state: 8 (over z, core).
Axes of the slice: x: 2, y: 2, z: 4, core: 2. Of those that a mesh axis runs over, the one named last changes fastest.
Arguments:
- alpha_init: bfloat16 [32, 1024, 1024], P('dp', 'state'), may hold values from 0.099609375 to 4
- tokens: int32 [32, 3], P('dp'), may hold values from 0 to 511
- trans_rows: bfloat16 [1024, 1024], replicated, may hold values from 5e-05 to 1.11, as said below
- trans_cols: bfloat16 [1024, 1024], replicated, may hold values from 5e-05 to 1.11, as said below
- emit_rows: bfloat16 [512, 1024], replicated, may hold values from 0.001 to 1, as said below
- emit_cols: bfloat16 [512, 1024], replicated, may hold values from 0.001 to 1, as said below
- backward: bfloat16 [3, 32, 1024, 1024], P(None, 'dp', None, 'state'), may hold values from 0.2 to 32, as said below
Outputs:
- alpha_final: bfloat16 [32, 1024, 1024], P('dp', 'state')
- counts_rows: float32 [1024, 1024], P(None, ('dp', 'state'))
- counts_cols: float32 [1024, 1024], P(None, ('dp', 'state'))
- loglik: float32 [32], P('dp')
Inputs may be any that keep to these rules, and one draw needn't show every extreme that they name: `trans_rows`: positive transition weights. `trans_cols`: positive transition weights. `emit_rows`: positive emission weights. `emit_cols`: positive emission weights. Positive backward weights.
All inputs are finite; a program needn't handle non-finite values.
Results may differ from a plain program's by a relative error of at most 0.0046.
Values may be sent and summed in bfloat16 or wider, within the bound.
A program may use at most 128 MiB of HBM per device.

v0:
```python
import jax
import jax.numpy as jnp
from jax import lax
from jax.sharding import PartitionSpec as P

STEPS = 3


def on_device(alpha_init, tokens, trans_rows, trans_cols, emit_rows, emit_cols, backward):
    f32 = jnp.float32
    groups = lax.axis_size("state")
    seq_dev = alpha_init.shape[0]
    width_rows = trans_rows.shape[0]
    width_cols = trans_cols.shape[0]
    cols_dev = width_cols // groups
    offset = lax.axis_index("state") * cols_dev
    alpha = alpha_init
    sums_rows = jnp.zeros((width_rows, width_rows), f32)
    sums_cols = jnp.zeros((width_cols, width_cols), f32)
    loglik = jnp.zeros((seq_dev,), f32)
    for step in range(STEPS):
        tok = tokens[:, step]
        first = jnp.take(emit_rows, tok, axis=0).astype(f32)
        second_all = jnp.take(emit_cols, tok, axis=0)
        second = lax.dynamic_slice_in_dim(second_all, offset, cols_dev, 1).astype(f32)
        mixed = jnp.einsum("sij,jk->sik", alpha, trans_cols, preferred_element_type=f32).astype(
            jnp.bfloat16
        )
        mixed_cols = lax.all_to_all(mixed, "state", split_axis=2, concat_axis=1, tiled=True)
        moved = jnp.einsum("sik,il->slk", mixed_cols, trans_rows, preferred_element_type=f32)
        emission = first[:, :, None] * second[:, None, :]
        scaled = moved * emission
        total = lax.psum(jnp.sum(scaled, axis=(1, 2)), "state")
        norm = total / (width_rows * width_cols)
        weight = (emission * backward[step].astype(f32) / norm[:, None, None]).astype(jnp.bfloat16)
        pulled = jnp.einsum("il,slk->sik", trans_rows, weight, preferred_element_type=f32).astype(
            jnp.bfloat16
        )
        pulled_local = lax.all_to_all(pulled, "state", split_axis=1, concat_axis=2, tiled=True)
        sums_rows = sums_rows + jnp.einsum(
            "sik,slk->il", mixed_cols, weight, preferred_element_type=f32
        )
        sums_cols = sums_cols + jnp.einsum(
            "sij,sik->jk", alpha, pulled_local, preferred_element_type=f32
        )
        loglik = loglik + jnp.log(norm)
        fresh = (scaled / norm[:, None, None]).astype(jnp.bfloat16)
        alpha = lax.all_to_all(fresh, "state", split_axis=1, concat_axis=2, tiled=True)
    factor = 1.0 / (seq_dev * lax.axis_size("dp") * STEPS)
    terms_rows = trans_rows.astype(f32) * sums_rows * factor
    terms_cols = trans_cols.astype(f32) * sums_cols * factor
    counts_rows, counts_cols = (
        lax.psum_scatter(terms_rows, ("dp", "state"), scatter_dimension=1, tiled=True),
        lax.psum_scatter(terms_cols, ("dp", "state"), scatter_dimension=1, tiled=True),
    )
    return (alpha, counts_rows, counts_cols, loglik)


def solution(mesh):
    return jax.shard_map(
        on_device,
        mesh=mesh,
        in_specs=(
            P("dp", "state", None),
            P("dp", None),
            P(),
            P(),
            P(),
            P(),
            P(None, "dp", None, "state"),
        ),
        out_specs=(
            P("dp", "state", None),
            P(None, ("dp", "state")),
            P(None, ("dp", "state")),
            P("dp"),
        ),
        check_vma=False,
    )
```

profile of v0, /device:TPU:0, one launch (start us, length us, event | category | flops | bytes accessed | tf_op | source)
XLA Modules:
  0.0 794.2 jit_solution(109715956263950396)
XLA Ops:
  8.8 5.2 fusion.32
  14.0 4.1 copy.31
  18.1 6.5 all-to-all-start
  28.7 45.1 %all-to-all-done = bf16[8,128,1024]{1,0,2:T(8,128)(2,1)} async-done(((bf16[8,128,1024]{1,0,2:T(8,128)(2,1)}), bf16[8,128,1024]{1,0,2:T(8,128)(2,1)}, u32[]{:S(2)}, u32[]{:S(2)}) %all-to-all-start) | async-done | bytes 2097184 | tf_op jit(solution)/shard_map/all_to_all | solution.py:29
  73.8 4.3 copy.78
  78.0 4.2 all_to_all.120
  82.2 6.5 fusion.11
  88.7 14.5 %psum.21 = f32[8]{0:T(128)S(1)} all-reduce(f32[8]{0:T(128)S(1)} %get-tuple-element.20), channel_id=1, replica_groups=mesh['dp'=4,'state'=8] {'state'}, use_global_device_ids=true, to_apply=%region_1.3 | all-reduce | flops 8 | bytes 64 | tf_op jit(solution)/shard_map/psum | solution.py:33
  103.2 4.1 divide_convert_fusion.2
  107.3 4.1 copy.33
  111.4 52.6 %all_to_all.162 = bf16[8,1024,128]{2,0,1:T(8,128)(2,1)S(1)} all-to-all(bf16[8,1024,128]{2,0,1:T(8,128)(2,1)} %copy.33), channel_id=1, replica_groups=mesh['dp'=4,'state'=8] {'state'}, dimensions={1} | all-to-all | bytes 4194304 | tf_op jit(solution)/shard_map/all_to_all | solution.py:48
  166.7 4.1 all_to_all.124
  170.8 5.9 fusion.35
  176.7 4.1 copy.35
  180.8 15.7 %all-to-all-start.2 = ((bf16[8,128,1024]{1,0,2:T(8,128)(2,1)}), bf16[8,128,1024]{1,0,2:T(8,128)(2,1)}, u32[]{:S(2)}, u32[]{:S(2)}) async-start(bf16[8,128,1024]{1,0,2:T(8,128)(2,1)} %copy.35), calls=%async_computation.2 | async-start | bytes 4194304 | tf_op jit(solution)/shard_map/all_to_all | solution.py:29
  200.6 44.7 %all-to-all-done.2 = bf16[8,128,1024]{1,0,2:T(8,128)(2,1)} async-done(((bf16[8,128,1024]{1,0,2:T(8,128)(2,1)}), bf16[8,128,1024]{1,0,2:T(8,128)(2,1)}, u32[]{:S(2)}, u32[]{:S(2)}) %all-to-all-start.2) | async-done | bytes 2097184 | tf_op jit(solution)/shard_map/all_to_all | solution.py:29
  245.4 4.3 copy.76
  249.6 4.2 all_to_all.128
  253.8 6.5 fusion.12
  260.3 14.5 %psum.22 = f32[8]{0:T(128)S(1)} all-reduce(f32[8]{0:T(128)S(1)} %get-tuple-element.22), channel_id=1, replica_groups=mesh['dp'=4,'state'=8] {'state'}, use_global_device_ids=true, to_apply=%region_3.5 | all-reduce | flops 8 | bytes 64 | tf_op jit(solution)/shard_map/psum | solution.py:33
  274.8 4.1 divide_convert_fusion.1
  278.8 4.1 copy.37
  283.0 52.6 %all_to_all.163 = bf16[8,1024,128]{2,0,1:T(8,128)(2,1)S(1)} all-to-all(bf16[8,1024,128]{2,0,1:T(8,128)(2,1)} %copy.37), channel_id=1, replica_groups=mesh['dp'=4,'state'=8] {'state'}, dimensions={1} | all-to-all | bytes 4194304 | tf_op jit(solution)/shard_map/all_to_all | solution.py:48
  338.2 4.2 all_to_all.132
  342.4 5.9 fusion.38
  348.2 4.1 copy.39
  352.4 4.3 all-to-all-start.4
  360.6 4.0 copy.43
  364.6 5.7 fusion.58
  370.3 3.9 copy.67
  374.2 3.9 copy.66
  378.1 3.9 copy.68
  382.1 5.9 convert_bitcast_fusion.2
  388.1 4.1 copy.54
  392.2 6.7 fusion.56
  398.9 6.9 all-to-all-done.4
  405.8 4.4 all-to-all-start.6
  410.6 6.7 fusion.53
  417.3 4.3 copy.74
  421.5 4.2 all_to_all.136
  425.7 6.5 fusion.13
  432.2 24.3 %psum.23 = f32[8]{0:T(128)S(1)} all-reduce(f32[8]{0:T(128)S(1)} %get-tuple-element.24), channel_id=1, replica_groups=mesh['dp'=4,'state'=8] {'state'}, use_global_device_ids=true, to_apply=%region_5.7 | all-reduce | flops 8 | bytes 64 | tf_op jit(solution)/shard_map/psum | solution.py:33
  457.1 10.1 %fusion.10 = f32[1024,1024]{0,1:T(8,128)} fusion(f32[1024,1024,1]{0,1,2:T(8,128)} %fusion.53, f32[1024,1024,1]{0,1,2:T(8,128)} %fusion.56, bf16[1024,1024]{0,1:T(8,128)(2,1)} %copy.43, bf16[8,1024,128]{1,2,0:T(8,128)(2,1)} %all_to_all.136, bf16[1,8,1024,128]{2,3,1,0:T(8,128)(2,1)} %copy.68, f32[8]{0:T(128)S(1)} %get-tuple-element.19, ...), kind=kOutput, calls=%fused_computation.24 | convolution fusion | flops 2157969408 | bytes 18911264 | tf_op jit(solution)/shard_map/sik,slk->il/dot_general | solution.py:40
  467.1 5.9 convert_bitcast_fusion.1
  473.1 4.2 copy.56
  477.3 11.4 %all-to-all-start.7 = ((bf16[8,1024,128]{2,0,1:T(8,128)(2,1)}), bf16[8,1024,128]{2,0,1:T(8,128)(2,1)}, u32[]{:S(2)}, u32[]{:S(2)}) async-start(bf16[8,1024,128]{2,0,1:T(8,128)(2,1)} %copy.56), calls=%async_computation.8 | async-start | bytes 4194304 | tf_op jit(solution)/shard_map/all_to_all | solution.py:39
  488.7 6.0 convert_bitcast_fusion
  494.7 4.2 copy.58
  498.9 57.9 %all-to-all-done.7 = bf16[8,1024,128]{2,0,1:T(8,128)(2,1)} async-done(((bf16[8,1024,128]{2,0,1:T(8,128)(2,1)}), bf16[8,1024,128]{2,0,1:T(8,128)(2,1)}, u32[]{:S(2)}, u32[]{:S(2)}) %all-to-all-start.7) | async-done | bytes 2097184 | tf_op jit(solution)/shard_map/all_to_all | solution.py:39
  556.8 4.4 all-to-all-start.8
  561.2 3.9 copy.53
  565.2 4.1 copy.55
  569.3 5.5 fusion.59
  574.8 4.1 copy.57
  578.9 6.5 fusion.60
  585.4 40.8 %all-to-all-done.8 = bf16[8,1024,128]{2,0,1:T(8,128)(2,1)} async-done(((bf16[8,1024,128]{2,0,1:T(8,128)(2,1)}), bf16[8,1024,128]{2,0,1:T(8,128)(2,1)}, u32[]{:S(2)}, u32[]{:S(2)}) %all-to-all-start.8) | async-done | bytes 2097184 | tf_op jit(solution)/shard_map/all_to_all | solution.py:39
  626.3 4.1 copy.59
  630.4 9.7 %fusion.8 = f32[1024,1024]{0,1:T(8,128)} fusion(f32[1024,1024,1]{1,0,2:T(8,128)} %fusion.59, f32[1024,1024,1]{0,1,2:T(8,128)} %fusion.60, bf16[1024,1024]{0,1:T(8,128)(2,1)} %copy.53, bf16[8,128,1024]{1,2,0:T(8,128)(2,1)} %bitcast.180, bf16[8,128,1024]{2,1,0:T(8,128)(2,1)} %all_to_all.132), kind=kOutput, calls=%fused_computation.21 | convolution fusion | flops 2152726528 | bytes 18874368 | tf_op jit(solution)/shard_map/sij,sik->jk/dot_general | solution.py:43
  640.1 4.1 divide_convert_fusion
  644.2 4.1 copy.41
  648.4 74.3 %all_to_all.164 = bf16[8,1024,128]{2,0,1:T(8,128)(2,1)S(1)} all-to-all(bf16[8,1024,128]{2,0,1:T(8,128)(2,1)} %copy.41), channel_id=1, replica_groups=mesh['dp'=4,'state'=8] {'state'}, dimensions={1} | all-to-all | bytes 4194304 | tf_op jit(solution)/shard_map/all_to_all | solution.py:48
  722.7 2.7 copy.42
  725.4 4.2 all_to_all.140
  729.5 57.7 %reduce-scatter.5.cloned.1.call-done = f32[1024,32]{0,1:T(8,128)} async-done(((f32[1024,1024]{0,1:T(8,128)}), f32[1024,32]{0,1:T(8,128)}) %reduce-scatter.5.cloned.1.call-update) | async-done | bytes 131088 | tf_op jit(solution)/shard_map/reduce_scatter | solution.py:54
  (30 shorter events, 20.1 us)
Async XLA Ops:
  7.2 1.6 copy-start
  18.1 6.5 copy-start.1
  18.1 55.6 %all-to-all-start = ((bf16[8,128,1024]{1,0,2:T(8,128)(2,1)}), bf16[8,128,1024]{1,0,2:T(8,128)(2,1)}, u32[]{:S(2)}, u32[]{:S(2)}) async-start(bf16[8,128,1024]{1,0,2:T(8,128)(2,1)} %copy.31), calls=%async_computation | async-start | bytes 4194304 | tf_op jit(solution)/shard_map/all_to_all | solution.py:29
  180.8 64.5 %all-to-all-start.2 = ((bf16[8,128,1024]{1,0,2:T(8,128)(2,1)}), bf16[8,128,1024]{1,0,2:T(8,128)(2,1)}, u32[]{:S(2)}, u32[]{:S(2)}) async-start(bf16[8,128,1024]{1,0,2:T(8,128)(2,1)} %copy.35), calls=%async_computation.2 | async-start | bytes 4194304 | tf_op jit(solution)/shard_map/all_to_all | solution.py:29
  352.4 53.4 %all-to-all-start.4 = ((bf16[8,128,1024]{1,0,2:T(8,128)(2,1)}), bf16[8,128,1024]{1,0,2:T(8,128)(2,1)}, u32[]{:S(2)}, u32[]{:S(2)}) async-start(bf16[8,128,1024]{1,0,2:T(8,128)(2,1)} %copy.39), calls=%async_computation.4 | async-start | bytes 4194304 | tf_op jit(solution)/shard_map/all_to_all | solution.py:29
  405.8 71.5 %all-to-all-start.6 = ((bf16[8,1024,128]{2,0,1:T(8,128)(2,1)}), bf16[8,1024,128]{2,0,1:T(8,128)(2,1)}, u32[]{:S(2)}, u32[]{:S(2)}) async-start(bf16[8,1024,128]{2,0,1:T(8,128)(2,1)} %copy.54), calls=%async_computation.7 | async-start | bytes 4194304 | tf_op jit(solution)/shard_map/all_to_all | solution.py:39
  410.2 319.4 %reduce-scatter.3.cloned.1.call-start = ((), (), s32[]{:S(2)}) async-start(), calls=%async_computation.11 | async-start | bytes 4325376 | tf_op jit(solution)/shard_map/reduce_scatter | solution.py:53
  477.3 79.6 %all-to-all-start.7 = ((bf16[8,1024,128]{2,0,1:T(8,128)(2,1)}), bf16[8,1024,128]{2,0,1:T(8,128)(2,1)}, u32[]{:S(2)}, u32[]{:S(2)}) async-start(bf16[8,1024,128]{2,0,1:T(8,128)(2,1)} %copy.56), calls=%async_computation.8 | async-start | bytes 4194304 | tf_op jit(solution)/shard_map/all_to_all | solution.py:39
  556.8 69.4 %all-to-all-start.8 = ((bf16[8,1024,128]{2,0,1:T(8,128)(2,1)}), bf16[8,1024,128]{2,0,1:T(8,128)(2,1)}, u32[]{:S(2)}, u32[]{:S(2)}) async-start(bf16[8,1024,128]{2,0,1:T(8,128)(2,1)} %copy.58), calls=%async_computation.9 | async-start | bytes 4194304 | tf_op jit(solution)/shard_map/all_to_all | solution.py:39
  561.2 226.0 %reduce-scatter.5.cloned.1.call-start = ((), (), s32[]{:S(2)}) async-start(), calls=%async_computation.12 | async-start | bytes 4325376 | tf_op jit(solution)/shard_map/reduce_scatter | solution.py:54
Sparse Core Ops, SparseCore 0:
  467.3 160.1 reduce-scatter.2
  640.3 146.8 reduce-scatter.4
where the time goes:
time: 800 us; the launch traced here: 794 us
  waiting for transfers between devices  253 us (32%)
  blocking collectives  233 us (29%)
  local copies, waits for them, and re-layouts  134 us (17%)
  matrix products  99.5 us (12%)
  starting transfers between devices  47.2 us (6%)
  between operations  14.4 us (2%)
  other arithmetic  13.2 us (2%)
    all_to_all x3, blocking collectives, on_device(): lax.all_to_all(fresh, 'state', split_axis=1, concat_axis=2, tiled=True)  179 us
    all_to_all x3, waiting for transfers between devices, on_device(): lax.all_to_all(pulled, 'state', split_axis=1, concat_axis=2, tiled=True)  98.8 us
    all_to_all x3, waiting for transfers between devices, on_device(): lax.all_to_all(mixed, 'state', split_axis=2, concat_axis=1, tiled=True)  96.7 us
    reduce_scatter x1, waiting for transfers between devices, on_device(): lax.psum_scatter(terms_cols, ('dp', 'state'), scatter_dimension=1, tiled=...  57.7 us
    psum x3, blocking collectives, on_device(): total = lax.psum(jnp.sum(scaled, axis=(1, 2)), 'state')  53.3 us
    all_to_all x3, starting transfers between devices, on_device(): lax.all_to_all(mixed, 'state', split_axis=2, concat_axis=1, tiled=True)  26.5 us
    all_to_all x6, local copies, waits for them, and re-layouts, on_device(): lax.all_to_all(mixed, 'state', split_axis=2, concat_axis=1, tiled=True)  25.3 us
    dot_general x3, matrix products, on_device(): jnp.einsum('sik,slk->il', mixed_cols, weight, preferred_element_type=f32)  23.4 us
  transfers between devices with their start and end apart: 8, of which 6 were waited for; matrix products, arithmetic and copies ran while one was open for 19% of the time, Pallas kernels for 0%

commit v1 on v0

v1 whole, which is shorter than its diff:
```python
import functools

import jax
import jax.numpy as jnp
from jax import lax
from jax.experimental import pallas as pl
from jax.experimental.pallas import tpu as pltpu
from jax.sharding import PartitionSpec as P

STEPS = 3
F32 = jnp.float32
BF16 = jnp.bfloat16
NN = (((1,), (0,)), ((), ()))
NT = (((1,), (1,)), ((), ()))
TN = (((0,), (0,)), ((), ()))


def dot(a, b, dims=NN):
    return lax.dot_general(a, b, dims, preferred_element_type=F32)


def sequence_kernel(
    first_call,
    alpha_ref,
    rows_ref,
    rows_t_ref,
    cols_ref,
    rows_own_ref,
    cols_own_ref,
    back_mine_ref,
    back_other_ref,
    emit_l_ref,
    emit_k_ref,
    emit_l_own_ref,
    emit_k_own_ref,
    sum_l_ref,
    sum_k_ref,
    *rest,
):
    if first_call:
        final_ref, counts_r_ref, counts_c_ref, norm_ref = rest[:4]
    else:
        prev_r_ref, prev_c_ref, final_ref, counts_r_ref, counts_c_ref, norm_ref = rest[:6]
    ping, pong, mixed, mixed_own, weight, pulled = rest[-6:]
    width = alpha_ref.shape[0]
    cells = width * cols_ref.shape[1]
    half = back_mine_ref.shape[-1]
    tile = 256
    tiles = width // tile
    messages = (alpha_ref, ping, pong)
    for step in range(STEPS):
        alpha = messages[step]
        last = step == STEPS - 1
        v_row = sum_k_ref[step : step + 1, :]

        def mix(i, total, alpha=alpha, last=last, step=step, v_row=v_row):
            at = pl.ds(pl.multiple_of(i * tile, tile), tile)
            block = alpha[at, :]
            mixed_own[at, :] = dot(block, cols_own_ref[...]).astype(BF16)
            if not last:
                mixed[at, :] = dot(block, cols_ref[...]).astype(BF16)
            part = jnp.sum(block.astype(F32) * v_row, axis=1, keepdims=True)
            return total + jnp.sum(part * sum_l_ref[at, step : step + 1], axis=0, keepdims=True)

        total = lax.fori_loop(0, tiles, mix, jnp.zeros((1, 1), F32))
        norm = total / cells
        inv = 1.0 / norm
        norm_ref[step : step + 1, :] = jnp.broadcast_to(norm, (1, norm_ref.shape[1]))
        scaled_k = emit_k_own_ref[step : step + 1, :] * inv

        def weigh(i, carry, step=step, scaled_k=scaled_k):
            at = pl.ds(pl.multiple_of(i * tile, tile), tile)
            gain = emit_l_ref[at, step : step + 1]
            weight[at, :half] = (
                back_mine_ref[step, 0, at, :].astype(F32) * (gain * scaled_k[:, :half])
            ).astype(BF16)
            weight[at, half:] = (
                back_other_ref[step, 0, at, :].astype(F32) * (gain * scaled_k[:, half:])
            ).astype(BF16)
            return carry

        lax.fori_loop(0, tiles, weigh, 0)

        if not last:
            fresh = messages[step + 1]
            row_k = emit_k_ref[step : step + 1, :] * inv

            def move(i, carry, fresh=fresh, row_k=row_k, step=step):
                at = pl.ds(pl.multiple_of(i * tile, tile), tile)
                moved = dot(rows_t_ref[at, :], mixed[...])
                fresh[at, :] = (moved * (emit_l_ref[at, step : step + 1] * row_k)).astype(BF16)
                return carry

            lax.fori_loop(0, tiles, move, 0)
        else:
            held = dot(rows_own_ref[...], alpha[...]).astype(BF16)
            moved = dot(held, cols_ref[...])
            row_k = emit_k_ref[step : step + 1, :] * inv
            final_ref[...] = (moved * (emit_l_own_ref[:, step : step + 1] * row_k)).astype(BF16)

        def count(i, carry, step=step):
            at = pl.ds(pl.multiple_of(i * tile, tile), tile)
            pulled[at, :] = dot(rows_ref[at, :], weight[...]).astype(BF16)
            term = dot(weight[at, :], mixed_own[...], NT)
            if step > 0:
                counts_r_ref[at, :] += term
            elif first_call:
                counts_r_ref[at, :] = term
            else:
                counts_r_ref[at, :] = prev_r_ref[at, :] + term
            return carry

        lax.fori_loop(0, tiles, count, 0)
        term = dot(pulled[...], alpha[...], TN)
        if step > 0:
            counts_c_ref[...] += term
        elif first_call:
            counts_c_ref[...] = term
        else:
            counts_c_ref[...] = prev_c_ref[...] + term


def run_sequence(index, alpha, shared, back_mine, back_other, emits, previous):
    rows, rows_t, cols, rows_own, cols_own = shared
    width = alpha.shape[0]
    cols_all = cols.shape[1]
    own_rows = rows_own.shape[0]
    own_cols = cols_own.shape[1]
    half = back_mine.shape[-1]

    def whole(array):
        return pl.BlockSpec(array.shape, lambda i, n=array.ndim: (0,) * n)

    back_spec = pl.BlockSpec((STEPS, 1, width, half), lambda i: (0, index, 0, 0))
    operands = [alpha, rows, rows_t, cols, rows_own, cols_own, back_mine, back_other, *emits, *previous]
    specs = [whole(a) for a in operands]
    specs[6] = specs[7] = back_spec
    outs = [
        jax.ShapeDtypeStruct((own_rows, cols_all), BF16),
        jax.ShapeDtypeStruct((width, width), F32),
        jax.ShapeDtypeStruct((own_cols, cols_all), F32),
        jax.ShapeDtypeStruct((STEPS, 128), F32),
    ]
    flops = 2 * width * cols_all * (4 * width + 3 * 4 * own_cols + 2 * own_rows)
    return pl.pallas_call(
        functools.partial(sequence_kernel, not previous),
        grid=(1,),
        out_shape=outs,
        in_specs=[
            pl.BlockSpec(s.block_shape, s.index_map, pipeline_mode=pl.Buffered(1)) for s in specs
        ],
        out_specs=[whole(a) for a in outs],
        scratch_shapes=[
            pltpu.VMEM((width, cols_all), BF16),
            pltpu.VMEM((width, cols_all), BF16),
            pltpu.VMEM((width, cols_all), BF16),
            pltpu.VMEM((width, own_cols), BF16),
            pltpu.VMEM((width, own_cols), BF16),
            pltpu.VMEM((width, own_cols), BF16),
        ],
        compiler_params=pltpu.CompilerParams(vmem_limit_bytes=56 * 1024 * 1024),
        cost_estimate=pl.CostEstimate(flops=flops, bytes_accessed=24 * 1024 * 1024, transcendentals=0),
    )(*operands)


def on_device(alpha_init, tokens, trans_rows, trans_cols, emit_rows, emit_cols, backward):
    groups = lax.axis_size("state")
    dp = lax.axis_size("dp")
    me = lax.axis_index("state")
    core = me % 2
    seq_dev, rows_dev, width_cols = alpha_init.shape
    width_rows = trans_rows.shape[0]
    cols_dev = width_cols // groups
    half = seq_dev // 2
    pairs = [(d, d ^ 1) for d in range(groups)]
    lines = [list(range(c, groups, 2)) for c in range(2)]

    def swap(x):
        return lax.ppermute(x, "state", pairs)

    def split(x, axis):
        mine = lax.dynamic_slice_in_dim(x, core * half, half, axis)
        return mine, lax.dynamic_slice_in_dim(x, (1 - core) * half, half, axis)

    alpha_mine, alpha_send = split(alpha_init, 0)
    alpha_other = swap(alpha_send)
    chip_rows = jnp.where(
        core == 0,
        jnp.concatenate([alpha_mine, alpha_other], 1),
        jnp.concatenate([alpha_other, alpha_mine], 1),
    )
    back_mine, back_send = split(backward, 1)
    back_other = swap(back_send)

    def own(x, size, axis):
        return jnp.concatenate(
            [
                lax.dynamic_slice_in_dim(x, me * size, size, axis),
                lax.dynamic_slice_in_dim(x, (me + 1 - 2 * core) * size, size, axis),
            ],
            axis,
        )

    rows_t = trans_rows.T
    shared = (trans_rows, rows_t, trans_cols, own(rows_t, rows_dev, 0), own(trans_cols, cols_dev, 1))
    tok = lax.dynamic_slice_in_dim(tokens, core * half, half, 0)
    first = jnp.take(emit_rows, tok, axis=0)
    second = jnp.take(emit_cols, tok, axis=0)
    sum_l = jnp.einsum("stl,il->sit", first, trans_rows, preferred_element_type=F32)
    sum_k = jnp.einsum("stk,jk->stj", second, trans_cols, preferred_element_type=F32)
    emit_l = jnp.swapaxes(first, 1, 2).astype(F32)
    emit_k = second.astype(F32)
    emit_l_own = own(emit_l, rows_dev, 1)
    emit_k_own = own(emit_k, cols_dev, 2)

    previous = ()
    finals, norms = [], []
    for s in range(half):
        alpha = lax.all_gather(chip_rows[s], "state", axis=0, tiled=True, axis_index_groups=lines)
        emits = [x[s] for x in (emit_l, emit_k, emit_l_own, emit_k_own, sum_l, sum_k)]
        final, terms_r, terms_c, norm = run_sequence(
            s, alpha, shared, back_mine, back_other, emits, previous
        )
        previous = (terms_r, terms_c)
        finals.append(final)
        norms.append(norm[:, 0])

    final = jnp.stack(finals)
    final_mine, final_other = final[:, :rows_dev], swap(final[:, rows_dev:])
    alpha_final = jnp.where(
        core == 0,
        jnp.concatenate([final_mine, final_other], 0),
        jnp.concatenate([final_other, final_mine], 0),
    )
    logs = jnp.sum(jnp.log(jnp.stack(norms)), axis=1)
    logs_other = swap(logs)
    loglik = jnp.where(
        core == 0, jnp.concatenate([logs, logs_other]), jnp.concatenate([logs_other, logs])
    )

    factor = 1.0 / (seq_dev * dp * STEPS)
    block = width_rows // (groups * dp)
    place = lax.axis_index("dp") * groups + me
    sums_r = lax.psum_scatter(terms_r, ("dp", "state"), scatter_dimension=0, tiled=True)
    counts_rows = (
        lax.dynamic_slice_in_dim(rows_t, place * block, block, 0).astype(F32) * sums_r * factor
    ).T
    mine_c = terms_c[:cols_dev] + swap(terms_c[cols_dev:])
    sums_c = lax.psum_scatter(mine_c, "dp", scatter_dimension=0, tiled=True)
    order = [(d * groups + g, g * dp + d) for d in range(dp) for g in range(groups)]
    sums_c = lax.ppermute(sums_c, ("dp", "state"), order)
    col_block = width_cols // (groups * dp)
    counts_cols = (
        lax.dynamic_slice_in_dim(trans_cols, place * col_block, col_block, 1).astype(F32)
        * sums_c.T
        * factor
    )
    return (alpha_final, counts_rows, counts_cols, loglik)


def solution(mesh):
    return jax.shard_map(
        on_device,
        mesh=mesh,
        in_specs=(
            P("dp", "state", None),
            P("dp", None),
            P(),
            P(),
            P(),
            P(),
            P(None, "dp", None, "state"),
        ),
        out_specs=(
            P("dp", "state", None),
            P(None, ("dp", "state")),
            P(None, ("dp", "state")),
            P("dp"),
        ),
        check_vma=False,
    )
```

time: 800 us -> 417 us (0.52)
  blocking collectives: 233 us -> 0 us
  Pallas kernels: 0 us -> 126 us
  local copies, waits for them, and re-layouts: 134 us -> 26.8 us
  matrix products: 99.5 us -> 1.96 us
  starting transfers between devices: 47.2 us -> 3.51 us
  waiting for transfers between devices: 253 us -> 233 us
    all_to_all x6 -> x0, waiting for transfers between devices: 195 us -> none  [the longest x3 98.8 us: on_device(): lax.all_to_all(pulled, 'state', split_axis=1, concat_axis=2, tiled=True)]
    all_to_all x3 -> x0, blocking collectives: 179 us -> none  [on_device(): lax.all_to_all(fresh, 'state', split_axis=1, concat_axis=2, tiled=True)]
    pallas_call x0 -> x4, Pallas kernels: none -> 126 us  [run_sequence(): pl.pallas_call(functools.partial(sequence_kernel, not previous), grid=(1,...]
    reduce_scatter x2, waiting for transfers between devices: 57.7 us -> 158 us  [the longest x1 141 us: on_device(): lax.psum_scatter(terms_r, ('dp', 'state'), scatter_dimension=0, tiled=True)]
    dot_general x15 -> x2, matrix products: 99.5 us -> 1.96 us  [the longest x1 1.25 us: on_device(): jnp.einsum('stl,il->sit', first, trans_rows, preferred_element_type=F32)]
    all_gather x0 -> x4, waiting for transfers between devices: none -> 68.4 us  [on_device(): lax.all_gather(chip_rows[s], 'state', axis=0, tiled=True, axis_index_grou...]
    all_to_all x15 -> x0, local copies, waits for them, and re-layouts: 58.1 us -> none  [the longest x6 25.3 us: on_device(): lax.all_to_all(mixed, 'state', split_axis=2, concat_axis=1, tiled=True)]
    psum x3 -> x0, blocking collectives: 53.3 us -> none  [on_device(): total = lax.psum(jnp.sum(scaled, axis=(1, 2)), 'state')]
  transfers between devices with their start and end apart: 8 -> 12, of which waited for: 6 -> 9; matrix products, arithmetic and copies ran while one was open for 19% -> 7% of each run, Pallas kernels for 0% -> 23%
where the time goes in v1:
time: 417 us
  waiting for transfers between devices  233 us (56%)
  Pallas kernels  126 us (30%)
  local copies, waits for them, and re-layouts  26.8 us (6%)
  between operations  14.4 us (3%)
  other arithmetic  11.4 us (3%)
    reduce_scatter x1, waiting for transfers between devices, on_device(): lax.psum_scatter(terms_r, ('dp', 'state'), scatter_dimension=0, tiled=True)  141 us
    pallas_call x4, Pallas kernels, run_sequence(): pl.pallas_call(functools.partial(sequence_kernel, not previous), grid=(1,...  126 us
    all_gather x4, waiting for transfers between devices, on_device(): lax.all_gather(chip_rows[s], 'state', axis=0, tiled=True, axis_index_grou...  68.4 us
    reduce_scatter x1, waiting for transfers between devices, on_device(): sums_c = lax.psum_scatter(mine_c, 'dp', scatter_dimension=0, tiled=True)  16.8 us
  transfers between devices with their start and end apart: 12, of which 9 were waited for; matrix products, arithmetic and copies ran while one was open for 7% of the time, Pallas kernels for 23%

profile of v1, /device:TPU:0, one launch (start us, length us, event | category | flops | bytes accessed | tf_op | source)
XLA Modules:
  0.0 416.7 jit_solution(4549200007019642988)
XLA Ops:
  7.3 2.8 constant_dynamic-slice_fusion.9
  10.1 0.5 collective-permute-start
  10.5 2.5 collective-permute-done
  13.0 1.0 maximum_select_fusion
  14.1 1.4 fusion.33
  15.5 0.7 all-gather.11.cloned.1.call-update
  16.3 6.1 %constant_dynamic-slice_fusion.4 = (bf16[3,4,1024,128]{3,2,1,0:T(8,128)(2,1)}, bf16[3,4,1024,128]{3,2,1,0:T(8,128)(2,1)}) fusion(bf16[3,8,1024,128]{3,2,1,0:T(8,128)(2,1)} %param.15, s32[]{:T(128)S(6)} %select_n.67, s32[]{:T(128)S(6)} %select_n.66), kind=kLoop, calls=%fused_computation.79 | loop fusion | bytes 12582920 | tf_op jit(solution)/shard_map/dynamic_slice | solution.py:183
  22.4 0.4 collective-permute-start.1
  22.9 0.1 compare_and_fusion
  23.0 0.1 copy.71
  23.1 0.1 reshape.37
  23.2 0.6 gather_fusion
  23.8 0.5 copy.72
  24.3 0.1 copy.70
  24.4 2.9 copy.67
  27.3 2.7 gather_fusion.1
  30.1 0.1 fusion.20
  30.2 0.6 fusion.25
  30.8 0.3 fusion.7
  31.2 1.5 copy-done.2
  32.7 0.1 constant_dynamic-slice_fusion.7
  32.8 0.8 fusion.13
  33.6 0.9 pad_maximum_fusion.1.rows_own_ref
  34.5 0.9 pad_maximum_fusion.2.cols_own_ref
  35.4 0.7 fusion
  36.1 0.7 slice_bitcast_fusion.14
  36.8 1.3 fusion.4
  38.0 2.1 slice_bitcast_fusion.6
  40.2 0.2 reduce-scatter.5.cloned.1.call-start
  40.4 23.7 %all-gather.9.cloned.1.call-done = bf16[1,1024,1024]{2,1,0:T(8,128)(2,1)} async-done(((bf16[1,256,1024]{2,1,0:T(8,128)(2,1)}), bf16[1,1024,1024]{2,1,0:T(8,128)(2,1)}) %all-gather.9.cloned.1.call-update) | async-done | bytes 2097168 | tf_op jit(solution)/shard_map/all_gather | solution.py:219
  64.2 30.2 %shard_map.102 = (bf16[256,1024]{1,0:T(8,128)(2,1)}, f32[1024,1024]{1,0:T(8,128)}, f32[256,1024]{1,0:T(8,128)}, f32[3,128]{1,0:T(4,128)}) custom-call(bf16[1024,1024]{1,0:T(8,128)(2,1)} %bitcast.107, bf16[1024,1024]{1,0:T(8,128)(2,1)} %rows_ref.7, bf16[1024,1024]{1,0:T(8,128)(2,1)} %bitcast.93, bf16[1024,1024]{1,0:T(8,128)(2,1)} %cols_ref.7, ...), custom_call_target="tpu_custom_call" | custom-call | flops 16106127360 | bytes 25165824 | tf_op jit(solution)/shard_map/pallas_call | solution.py:145
  94.4 16.1 %all-gather.11.cloned.1.call-done = bf16[1,1024,1024]{2,1,0:T(8,128)(2,1)} async-done(((bf16[1,256,1024]{2,1,0:T(8,128)(2,1)}), bf16[1,1024,1024]{2,1,0:T(8,128)(2,1)}) %all-gather.11.cloned.1.call-update) | async-done | bytes 2097168 | tf_op jit(solution)/shard_map/all_gather | solution.py:219
  110.4 32.0 %shard_map.103 = (bf16[256,1024]{1,0:T(8,128)(2,1)}, f32[1024,1024]{1,0:T(8,128)}, f32[256,1024]{1,0:T(8,128)}, f32[3,128]{1,0:T(4,128)}) custom-call(bf16[1024,1024]{1,0:T(8,128)(2,1)} %bitcast.106, bf16[1024,1024]{1,0:T(8,128)(2,1)} %rows_ref.7, bf16[1024,1024]{1,0:T(8,128)(2,1)} %bitcast.94, bf16[1024,1024]{1,0:T(8,128)(2,1)} %cols_ref.7, ...), custom_call_target="tpu_custom_call" | custom-call | flops 16106127360 | bytes 25165824 | tf_op jit(solution)/shard_map/pallas_call | solution.py:145
  142.4 14.3 %all-gather.13.cloned.1.call-done = bf16[1,1024,1024]{2,1,0:T(8,128)(2,1)} async-done(((bf16[1,256,1024]{2,1,0:T(8,128)(2,1)}), bf16[1,1024,1024]{2,1,0:T(8,128)(2,1)}) %all-gather.13.cloned.1.call-update) | async-done | bytes 2097168 | tf_op jit(solution)/shard_map/all_gather | solution.py:219
  156.7 31.8 %shard_map.104 = (bf16[256,1024]{1,0:T(8,128)(2,1)}, f32[1024,1024]{1,0:T(8,128)}, f32[256,1024]{1,0:T(8,128)}, f32[3,128]{1,0:T(4,128)}) custom-call(bf16[1024,1024]{1,0:T(8,128)(2,1)} %bitcast.105, bf16[1024,1024]{1,0:T(8,128)(2,1)} %rows_ref.7, bf16[1024,1024]{1,0:T(8,128)(2,1)} %bitcast.95, bf16[1024,1024]{1,0:T(8,128)(2,1)} %cols_ref.7, ...), custom_call_target="tpu_custom_call" | custom-call | flops 16106127360 | bytes 25165824 | tf_op jit(solution)/shard_map/pallas_call | solution.py:145
  188.5 14.3 %all-gather.15.cloned.1.call-done = bf16[1,1024,1024]{2,1,0:T(8,128)(2,1)} async-done(((bf16[1,256,1024]{2,1,0:T(8,128)(2,1)}), bf16[1,1024,1024]{2,1,0:T(8,128)(2,1)}) %all-gather.15.cloned.1.call-update) | async-done | bytes 2097168 | tf_op jit(solution)/shard_map/all_gather | solution.py:219
  202.8 32.0 %shard_map.105 = (bf16[256,1024]{1,0:T(8,128)(2,1)}, f32[1024,1024]{1,0:T(8,128)}, f32[256,1024]{1,0:T(8,128)}, f32[3,128]{1,0:T(4,128)}) custom-call(bf16[1024,1024]{1,0:T(8,128)(2,1)} %bitcast.108, bf16[1024,1024]{1,0:T(8,128)(2,1)} %rows_ref.7, bf16[1024,1024]{1,0:T(8,128)(2,1)} %bitcast.96, bf16[1024,1024]{1,0:T(8,128)(2,1)} %cols_ref.7, ...), custom_call_target="tpu_custom_call" | custom-call | flops 16106127360 | bytes 25165824 | tf_op jit(solution)/shard_map/pallas_call | solution.py:145
  234.8 1.1 slice.139
  236.0 1.9 collective-permute-done.3
  237.9 1.9 slice_add_fusion
  239.9 0.5 reduce-scatter.3.cloned.1.call-update
  240.4 0.5 copy-done.5
  240.9 0.2 copy-done.6
  241.1 0.2 copy-done.7
  241.2 0.2 copy-done.8
  241.4 0.3 pad_maximum_fusion
  241.7 1.1 fusion.32
  242.9 0.1 collective-permute-start.2
  243.0 1.1 constant_dynamic-slice_fusion
  244.1 0.1 copy.88
  244.2 0.1 slice_reduce_fusion
  244.3 0.1 slice_reduce_fusion.1
  244.5 0.1 slice_reduce_fusion.2
  244.6 0.1 slice_reduce_fusion.3
  244.7 0.1 fusion.29
  244.8 0.4 collective-permute-start.5
  245.3 0.8 collective-permute-done.5
  246.1 0.6 broadcast_select_fusion.4
  246.7 16.8 %reduce-scatter.5.cloned.1.call-done = f32[32,1024]{1,0:T(8,128)} async-done(((f32[128,1024]{1,0:T(8,128)}), f32[32,1024]{1,0:T(8,128)}) %reduce-scatter.5.cloned.1.call-update) | async-done | bytes 131088 | tf_op jit(solution)/shard_map/reduce_scatter | solution.py:249
  263.5 1.6 collective-permute-start.4
  265.1 1.6 maximum_select_fusion.1
  266.7 0.7 fusion.17
  267.4 140.9 %reduce-scatter.3.cloned.1.call-done = f32[32,1024]{1,0:T(8,128)} async-done(((f32[1024,1024]{1,0:T(8,128)}), f32[32,1024]{1,0:T(8,128)}) %reduce-scatter.3.cloned.1.call-update) | async-done | bytes 131088 | tf_op jit(solution)/shard_map/reduce_scatter | solution.py:244
  408.3 1.6 fusion.19
  (42 shorter events, 0.6 us)
Async XLA Ops:
  7.2 16.0 %copy-start = (bf16[512,1024]{1,0:T(8,128)(2,1)S(1)}, bf16[512,1024]{1,0:T(8,128)(2,1)}, u32[]{:S(2)}) copy-start(bf16[512,1024]{1,0:T(8,128)(2,1)} %param.13) | copy-start | bytes 3145732
  7.2 57.0 %all-gather.9.cloned.1.call-start = ((), (), s32[]{:S(2)}) async-start(), calls=%async_computation.4 | async-start | bytes 2621440 | tf_op jit(solution)/shard_map/all_gather | solution.py:219
  10.1 3.0 collective-permute-start
  15.4 95.0 %all-gather.11.cloned.1.call-start = ((), (), s32[]{:S(2)}) async-start(), calls=%async_computation.5 | async-start | bytes 2621440 | tf_op jit(solution)/shard_map/all_gather | solution.py:219
  16.2 6.7 %copy-start.13 = (s32[8,3]{0,1:T(4,128)S(1)}, s32[8,3]{0,1:T(4,128)}, u32[]{:S(2)}) copy-start(s32[8,3]{0,1:T(4,128)} %param.10) | copy-start | bytes 292
  16.2 140.5 %all-gather.13.cloned.1.call-start = ((), (), s32[]{:S(2)}) async-start(), calls=%async_computation.6 | async-start | bytes 2621440 | tf_op jit(solution)/shard_map/all_gather | solution.py:219
  22.4 180.4 %all-gather.15.cloned.1.call-start = ((), (), s32[]{:S(2)}) async-start(), calls=%async_computation.7 | async-start | bytes 2621440 | tf_op jit(solution)/shard_map/all_gather | solution.py:219
  22.4 18.0 %collective-permute-start.1 = (bf16[3,4,1024,128]{3,2,1,0:T(8,128)(2,1)}, bf16[3,4,1024,128]{3,2,1,0:T(8,128)(2,1)}, u32[]{:S(2)}, u32[]{:S(2)}) collective-permute-start(bf16[3,4,1024,128]{3,2,1,0:T(8,128)(2,1)} %get-tuple-element.39), channel_id=1, source_target_pairs={{0,1},{1,0},{2,3},{3,2},{4,5},{5,4},{6,7},{7,6},{8,9},{9,8},{10,11... | collective-permute-start | bytes 9437192 | tf_op jit(solution)/shard_map/ppermute | solution.py:179
  27.3 3.8 copy-start.3
  31.1 1.6 copy-start.2
  33.6 3.2 copy-start.4
  40.2 223.3 %reduce-scatter.5.cloned.1.call-start = ((), (), s32[]{:S(2)}) async-start(), calls=%async_computation.3 | async-start | bytes 655360 | tf_op jit(solution)/shard_map/reduce_scatter | solution.py:249
  235.9 2.0 collective-permute-start.3
  239.8 168.4 %reduce-scatter.3.cloned.1.call-start = ((), (), s32[]{:S(2)}) async-start(), calls=%async_computation.2 | async-start | bytes 4325376 | tf_op jit(solution)/shard_map/reduce_scatter | solution.py:244
  239.9 1.0 copy-start.5
  239.9 1.2 copy-start.6
  239.9 1.3 copy-start.7
  239.9 1.5 copy-start.8
  241.7 2.5 copy-start.12
  241.7 2.6 copy-start.11
  241.7 2.8 copy-start.10
  241.7 2.9 copy-start.9
  242.9 22.2 %collective-permute-start.2 = (bf16[4,128,1024]{2,1,0:T(8,128)(2,1)}, bf16[4,128,1024]{2,1,0:T(8,128)(2,1)S(1)}, u32[]{:S(2)}, u32[]{:S(2)}) collective-permute-start(bf16[4,128,1024]{2,1,0:T(8,128)(2,1)} %get-tuple-element.42), channel_id=1, source_target_pairs={{0,1},{1,0},{2,3},{3,2},{4,5},{5,4},{6,7},{7,6},{8,9},{9,8},{10,11... | collective-permute-start | bytes 3145736 | tf_op jit(solution)/shard_map/ppermute | solution.py:179
  244.8 1.3 collective-permute-start.5
  263.5 3.2 collective-permute-start.4
  265.1 144.8 %copy-start.1 = (bf16[512,1024]{1,0:T(8,128)(2,1)S(1)}, bf16[512,1024]{1,0:T(8,128)(2,1)}, u32[]{:S(2)}) copy-start(bf16[512,1024]{1,0:T(8,128)(2,1)} %param.13) | copy-start | bytes 3145732
Sparse Core Ops, SparseCore 0:
  15.6 48.5 all-gather.8
  65.7 44.6 all-gather.10
  112.0 44.6 all-gather.12
  158.1 44.6 all-gather.14
  240.0 23.5 reduce-scatter.4
  265.7 142.4 reduce-scatter.2

commit v2 on v1

--- a/solution.py
+++ b/solution.py
@@ -239,17 +239,31 @@
     )
 
     factor = 1.0 / (seq_dev * dp * STEPS)
+    chips = groups // 2
     block = width_rows // (groups * dp)
+    col_block = width_cols // (groups * dp)
     place = lax.axis_index("dp") * groups + me
-    sums_r = lax.psum_scatter(terms_r, ("dp", "state"), scatter_dimension=0, tiled=True)
+    by_core = terms_r.reshape(dp, chips, 2, block, width_rows)
+
+    def of_core(c, cols):
+        rows = lax.dynamic_index_in_dim(by_core, c, 2, keepdims=False)
+        return jnp.concatenate(
+            [rows.reshape(dp, chips * block, width_rows), cols.reshape(dp, col_block, width_cols)], 1
+        )
+
+    here = of_core(core, terms_c[:cols_dev])
+    there = swap(of_core(1 - core, terms_c[cols_dev:]).astype(BF16))
+    both = (here + there.astype(F32)).astype(BF16)
+    parts = lax.all_to_all(both, "dp", 0, 0, tiled=True)
+    sums = jnp.sum(parts.astype(F32), axis=0)
+    order = [(d * groups + g, g * dp + d) for d in range(dp) for g in range(groups)]
+    sums_c = lax.ppermute(sums[chips * block :], ("dp", "state"), order)
+    line = sums[: chips * block].reshape(chips, block, width_rows).astype(BF16)
+    line = lax.all_to_all(line, "state", 0, 0, tiled=True, axis_index_groups=lines)
+    sums_r = jnp.sum(line.astype(F32), axis=0)
     counts_rows = (
         lax.dynamic_slice_in_dim(rows_t, place * block, block, 0).astype(F32) * sums_r * factor
     ).T
-    mine_c = terms_c[:cols_dev] + swap(terms_c[cols_dev:])
-    sums_c = lax.psum_scatter(mine_c, "dp", scatter_dimension=0, tiled=True)
-    order = [(d * groups + g, g * dp + d) for d in range(dp) for g in range(groups)]
-    sums_c = lax.ppermute(sums_c, ("dp", "state"), order)
-    col_block = width_cols // (groups * dp)
     counts_cols = (
         lax.dynamic_slice_in_dim(trans_cols, place * col_block, col_block, 1).astype(F32)
         * sums_c.T

time: 417 us -> 294 us (0.71)
  waiting for transfers between devices: 233 us -> 89.9 us
  starting transfers between devices: 3.51 us -> 13.7 us
  local copies, waits for them, and re-layouts: 26.8 us -> 31.9 us
  other arithmetic: 11.4 us -> 16 us
    reduce_scatter x2 -> x0, waiting for transfers between devices: 158 us -> none  [the longest x1 141 us: on_device(): lax.psum_scatter(terms_r, ('dp', 'state'), scatter_dimension=0, tiled=True)]
    all_to_all x0 -> x2, waiting for transfers between devices: none -> 16.5 us  [the longest x1 11.6 us: on_device(): parts = lax.all_to_all(both, 'dp', 0, 0, tiled=True)]
    all_to_all x0 -> x2, starting transfers between devices: none -> 10 us  [the longest x1 5.71 us: on_device(): lax.all_to_all(line, 'state', 0, 0, tiled=True, axis_index_groups=lines)]
  transfers between devices with their start and end apart: 12 -> 12, of which waited for: 9 -> 9; matrix products, arithmetic and copies ran while one was open for 7% -> 12% of each run, Pallas kernels for 23% -> 32%
where the time goes in v2:
time: 294 us
  Pallas kernels  126 us (43%)
  waiting for transfers between devices  89.9 us (31%)
  local copies, waits for them, and re-layouts  31.9 us (11%)
  other arithmetic  16 us (5%)
  between operations  14.1 us (5%)
  starting transfers between devices  13.7 us (5%)
    pallas_call x4, Pallas kernels, run_sequence(): pl.pallas_call(functools.partial(sequence_kernel, not previous), grid=(1,...  126 us
    all_gather x4, waiting for transfers between devices, on_device(): lax.all_gather(chip_rows[s], 'state', axis=0, tiled=True, axis_index_grou...  68.4 us
    all_to_all x1, waiting for transfers between devices, on_device(): parts = lax.all_to_all(both, 'dp', 0, 0, tiled=True)  11.6 us
    dynamic_slice x1, local copies, waits for them, and re-layouts, split(): return (mine, lax.dynamic_slice_in_dim(x, (1 - core) * half, half, axis))  6.11 us
  transfers between devices with their start and end apart: 12, of which 9 were waited for; matrix products, arithmetic and copies ran while one was open for 12% of the time, Pallas kernels for 32%

profile of v2, /device:TPU:0, one launch (start us, length us, event | category | flops | bytes accessed | tf_op | source)
XLA Modules:
  0.0 293.6 jit_solution(8106943519235714939)
XLA Ops:
  7.3 2.8 constant_dynamic-slice_fusion.10
  10.1 0.5 collective-permute-start
  10.5 2.5 collective-permute-done
  13.0 1.0 maximum_select_fusion
  14.1 1.4 fusion.33
  15.5 0.7 all-gather.11.cloned.1.call-update
  16.3 6.1 %constant_dynamic-slice_fusion.5 = (bf16[3,4,1024,128]{3,2,1,0:T(8,128)(2,1)}, bf16[3,4,1024,128]{3,2,1,0:T(8,128)(2,1)}) fusion(bf16[3,8,1024,128]{3,2,1,0:T(8,128)(2,1)} %param.15, s32[]{:T(128)S(6)} %select_n.74, s32[]{:T(128)S(6)} %select_n.73), kind=kLoop, calls=%fused_computation.77 | loop fusion | bytes 12582920 | tf_op jit(solution)/shard_map/dynamic_slice | solution.py:183
  22.4 0.4 collective-permute-start.1
  23.0 0.1 copy.71
  23.2 0.6 gather_fusion
  23.8 0.5 copy.72
  24.3 0.1 copy.70
  24.4 3.0 %copy.67 = bf16[1024,1024]{0,1:T(8,128)(2,1)S(1)} copy(bf16[1024,1024]{1,0:T(8,128)(2,1)} %rows_ref.7) | data formatting | bytes 4194304 | tf_op args[2]
  27.4 2.7 gather_fusion.1
  30.3 0.6 fusion.25
  30.9 0.3 fusion.8
  31.3 1.5 copy-done.3
  32.8 0.1 constant_dynamic-slice_fusion.8
  33.0 0.8 fusion.14
  33.8 0.9 pad_maximum_fusion.2.rows_own_ref
  34.6 0.9 pad_maximum_fusion.3.cols_own_ref
  35.5 0.7 fusion.1
  36.3 0.7 slice_bitcast_fusion.14
  36.9 1.3 fusion.5
  38.2 2.1 slice_bitcast_fusion.6
  40.3 23.8 %all-gather.9.cloned.1.call-done = bf16[1,1024,1024]{2,1,0:T(8,128)(2,1)} async-done(((bf16[1,256,1024]{2,1,0:T(8,128)(2,1)}), bf16[1,1024,1024]{2,1,0:T(8,128)(2,1)}) %all-gather.9.cloned.1.call-update) | async-done | bytes 2097168 | tf_op jit(solution)/shard_map/all_gather | solution.py:219
  64.2 30.2 %shard_map.102 = (bf16[256,1024]{1,0:T(8,128)(2,1)}, f32[1024,1024]{1,0:T(8,128)}, f32[256,1024]{1,0:T(8,128)}, f32[3,128]{1,0:T(4,128)}) custom-call(bf16[1024,1024]{1,0:T(8,128)(2,1)} %bitcast.115, bf16[1024,1024]{1,0:T(8,128)(2,1)} %rows_ref.7, bf16[1024,1024]{1,0:T(8,128)(2,1)} %bitcast.97, bf16[1024,1024]{1,0:T(8,128)(2,1)} %cols_ref.7, ...), custom_call_target="tpu_custom_call" | custom-call | flops 16106127360 | bytes 25165824 | tf_op jit(solution)/shard_map/pallas_call | solution.py:145
  94.4 16.1 %all-gather.11.cloned.1.call-done = bf16[1,1024,1024]{2,1,0:T(8,128)(2,1)} async-done(((bf16[1,256,1024]{2,1,0:T(8,128)(2,1)}), bf16[1,1024,1024]{2,1,0:T(8,128)(2,1)}) %all-gather.11.cloned.1.call-update) | async-done | bytes 2097168 | tf_op jit(solution)/shard_map/all_gather | solution.py:219
  110.5 32.0 %shard_map.103 = (bf16[256,1024]{1,0:T(8,128)(2,1)}, f32[1024,1024]{1,0:T(8,128)}, f32[256,1024]{1,0:T(8,128)}, f32[3,128]{1,0:T(4,128)}) custom-call(bf16[1024,1024]{1,0:T(8,128)(2,1)} %bitcast.114, bf16[1024,1024]{1,0:T(8,128)(2,1)} %rows_ref.7, bf16[1024,1024]{1,0:T(8,128)(2,1)} %bitcast.98, bf16[1024,1024]{1,0:T(8,128)(2,1)} %cols_ref.7, ...), custom_call_target="tpu_custom_call" | custom-call | flops 16106127360 | bytes 25165824 | tf_op jit(solution)/shard_map/pallas_call | solution.py:145
  142.5 14.1 %all-gather.13.cloned.1.call-done = bf16[1,1024,1024]{2,1,0:T(8,128)(2,1)} async-done(((bf16[1,256,1024]{2,1,0:T(8,128)(2,1)}), bf16[1,1024,1024]{2,1,0:T(8,128)(2,1)}) %all-gather.13.cloned.1.call-update) | async-done | bytes 2097168 | tf_op jit(solution)/shard_map/all_gather | solution.py:219
  156.6 31.8 %shard_map.104 = (bf16[256,1024]{1,0:T(8,128)(2,1)}, f32[1024,1024]{1,0:T(8,128)}, f32[256,1024]{1,0:T(8,128)}, f32[3,128]{1,0:T(4,128)}) custom-call(bf16[1024,1024]{1,0:T(8,128)(2,1)} %bitcast.113, bf16[1024,1024]{1,0:T(8,128)(2,1)} %rows_ref.7, bf16[1024,1024]{1,0:T(8,128)(2,1)} %bitcast.99, bf16[1024,1024]{1,0:T(8,128)(2,1)} %cols_ref.7, ...), custom_call_target="tpu_custom_call" | custom-call | flops 16106127360 | bytes 25165824 | tf_op jit(solution)/shard_map/pallas_call | solution.py:145
  188.4 14.3 %all-gather.15.cloned.1.call-done = bf16[1,1024,1024]{2,1,0:T(8,128)(2,1)} async-done(((bf16[1,256,1024]{2,1,0:T(8,128)(2,1)}), bf16[1,1024,1024]{2,1,0:T(8,128)(2,1)}) %all-gather.15.cloned.1.call-update) | async-done | bytes 2097168 | tf_op jit(solution)/shard_map/all_gather | solution.py:219
  202.8 32.1 %shard_map.105 = (bf16[256,1024]{1,0:T(8,128)(2,1)}, f32[1024,1024]{1,0:T(8,128)}, f32[256,1024]{1,0:T(8,128)}, f32[3,128]{1,0:T(4,128)}) custom-call(bf16[1024,1024]{1,0:T(8,128)(2,1)} %bitcast.116, bf16[1024,1024]{1,0:T(8,128)(2,1)} %rows_ref.7, bf16[1024,1024]{1,0:T(8,128)(2,1)} %bitcast.100, bf16[1024,1024]{1,0:T(8,128)(2,1)} %cols_ref.7, ...), custom_call_target="tpu_custom_call" | custom-call | flops 16106127360 | bytes 25165824 | tf_op jit(solution)/shard_map/pallas_call | solution.py:145
  234.8 1.1 slice.266
  235.9 1.8 dynamic-slice_convert_fusion
  237.8 1.2 pad_maximum_fusion.1
  239.0 1.9 constant_dynamic-slice_fusion.1
  241.0 0.2 copy-done.10
  241.1 0.3 pad_maximum_fusion
  241.4 0.9 collective-permute-done.3
  242.3 2.8 fusion
  245.1 4.3 %all-to-all-start = ((bf16[4,160,1024]{2,1,0:T(8,128)(2,1)}), bf16[4,160,1024]{2,1,0:T(8,128)(2,1)}, u32[]{:S(2)}, u32[]{:S(2)}) async-start(bf16[4,160,1024]{2,1,0:T(8,128)(2,1)} %fusion), calls=%async_computation | async-start | bytes 2621440 | tf_op jit(solution)/shard_map/all_to_all | solution.py:257
  249.5 1.6 fusion.32
  251.1 0.1 collective-permute-start.2
  251.2 1.2 constant_dynamic-slice_fusion
  252.4 0.1 copy.88
  252.5 0.1 slice_reduce_fusion
  252.6 0.1 slice_reduce_fusion.1
  252.8 0.1 slice_reduce_fusion.2
  252.9 0.1 slice_reduce_fusion.3
  253.0 0.1 fusion.29
  253.1 0.4 collective-permute-start.5
  253.5 0.8 collective-permute-done.5
  254.3 0.6 broadcast_select_fusion.4
  254.9 11.6 %all-to-all-done = bf16[4,160,1024]{2,1,0:T(8,128)(2,1)} async-done(((bf16[4,160,1024]{2,1,0:T(8,128)(2,1)}), bf16[4,160,1024]{2,1,0:T(8,128)(2,1)}, u32[]{:S(2)}, u32[]{:S(2)}) %all-to-all-start) | async-done | bytes 1310752 | tf_op jit(solution)/shard_map/all_to_all | solution.py:257
  266.5 1.6 convert_reduce_fusion
  268.2 0.7 slice.194
  268.8 0.7 slice.265
  269.5 2.1 collective-permute-start.4
  271.7 5.7 %all-to-all-start.1 = ((bf16[4,32,1024]{2,1,0:T(8,128)(2,1)}), bf16[4,32,1024]{2,1,0:T(8,128)(2,1)S(1)}, u32[]{:S(2)}, u32[]{:S(2)}) async-start(bf16[4,32,1024]{2,1,0:T(8,128)(2,1)} %bitcast.46), calls=%async_computation.1 | async-start | bytes 524288 | tf_op jit(solution)/shard_map/all_to_all | solution.py:262
  277.4 1.6 maximum_select_fusion.1
  279.1 1.6 fusion.18
  280.6 4.9 %all-to-all-done.1 = bf16[4,32,1024]{2,1,0:T(8,128)(2,1)S(1)} async-done(((bf16[4,32,1024]{2,1,0:T(8,128)(2,1)}), bf16[4,32,1024]{2,1,0:T(8,128)(2,1)S(1)}, u32[]{:S(2)}, u32[]{:S(2)}) %all-to-all-start.1) | async-done | bytes 262176 | tf_op jit(solution)/shard_map/all_to_all | solution.py:262
  285.6 1.5 fusion.19
  (52 shorter events, 0.8 us)
Async XLA Ops:
  7.2 16.0 %copy-start = (bf16[512,1024]{1,0:T(8,128)(2,1)S(1)}, bf16[512,1024]{1,0:T(8,128)(2,1)}, u32[]{:S(2)}) copy-start(bf16[512,1024]{1,0:T(8,128)(2,1)} %param.13) | copy-start | bytes 3145732
  7.2 57.0 %all-gather.9.cloned.1.call-start = ((), (), s32[]{:S(2)}) async-start(), calls=%async_computation.2 | async-start | bytes 2621440 | tf_op jit(solution)/shard_map/all_gather | solution.py:219
  10.1 3.0 %collective-permute-start = (bf16[4,128,1024]{2,1,0:T(8,128)(2,1)}, bf16[4,128,1024]{2,1,0:T(8,128)(2,1)S(1)}, u32[]{:S(2)}, u32[]{:S(2)}) collective-permute-start(bf16[4,128,1024]{2,1,0:T(8,128)(2,1)} %get-tuple-element.62), channel_id=1, source_target_pairs={{0,1},{1,0},{2,3},{3,2},{4,5},{5,4},{6,7},{7,6},{8,9},{9,8},{10,11... | collective-permute-start | bytes 3145736 | tf_op jit(solution)/shard_map/ppermute | solution.py:179
  15.4 95.0 %all-gather.11.cloned.1.call-start = ((), (), s32[]{:S(2)}) async-start(), calls=%async_computation.3 | async-start | bytes 2621440 | tf_op jit(solution)/shard_map/all_gather | solution.py:219
  16.2 6.7 %copy-start.15 = (s32[8,3]{0,1:T(4,128)S(1)}, s32[8,3]{0,1:T(4,128)}, u32[]{:S(2)}) copy-start(s32[8,3]{0,1:T(4,128)} %param.10) | copy-start | bytes 292
  16.2 140.4 %all-gather.13.cloned.1.call-start = ((), (), s32[]{:S(2)}) async-start(), calls=%async_computation.4 | async-start | bytes 2621440 | tf_op jit(solution)/shard_map/all_gather | solution.py:219
  22.4 180.4 %all-gather.15.cloned.1.call-start = ((), (), s32[]{:S(2)}) async-start(), calls=%async_computation.5 | async-start | bytes 2621440 | tf_op jit(solution)/shard_map/all_gather | solution.py:219
  22.4 17.9 %collective-permute-start.1 = (bf16[3,4,1024,128]{3,2,1,0:T(8,128)(2,1)}, bf16[3,4,1024,128]{3,2,1,0:T(8,128)(2,1)}, u32[]{:S(2)}, u32[]{:S(2)}) collective-permute-start(bf16[3,4,1024,128]{3,2,1,0:T(8,128)(2,1)} %get-tuple-element.39), channel_id=1, source_target_pairs={{0,1},{1,0},{2,3},{3,2},{4,5},{5,4},{6,7},{7,6},{8,9},{9,8},{10,11... | collective-permute-start | bytes 9437192 | tf_op jit(solution)/shard_map/ppermute | solution.py:179
  27.4 3.8 %copy-start.4 = (bf16[1024,1024]{0,1:T(8,128)(2,1)}, bf16[1024,1024]{0,1:T(8,128)(2,1)S(1)}, u32[]{:S(2)}) copy-start(bf16[1024,1024]{0,1:T(8,128)(2,1)S(1)} %copy.67) | copy-start | bytes 6291460
  31.2 1.6 copy-start.3
  33.8 3.2 %copy-start.5 = (bf16[1024,1024]{1,0:T(8,128)(2,1)S(1)}, bf16[1024,1024]{1,0:T(8,128)(2,1)}, u32[]{:S(2)}) copy-start(bf16[1024,1024]{1,0:T(8,128)(2,1)} %rows_ref.7) | copy-start | bytes 6291460
  235.9 3.0 %copy-start.6 = (f32[256,1024]{1,0:T(8,128)S(1)}, f32[256,1024]{1,0:T(8,128)}, u32[]{:S(2)}) copy-start(f32[256,1024]{1,0:T(8,128)} %get-tuple-element.32) | copy-start | bytes 3145732
  238.9 3.4 %collective-permute-start.3 = (bf16[4,160,1024]{2,1,0:T(8,128)(2,1)}, bf16[4,160,1024]{2,1,0:T(8,128)(2,1)}, u32[]{:S(2)}, u32[]{:S(2)}) collective-permute-start(bf16[4,160,1024]{2,1,0:T(8,128)(2,1)} %pad_maximum_fusion.1), channel_id=1, source_target_pairs={{0,1},{1,0},{2,3},{3,2},{4,5},{5,4},{6,7},{7,6},{8,9},{9,8},{10,11... | collective-permute-start | bytes 3932168 | tf_op jit(solution)/shard_map/ppermute | solution.py:179
  239.0 1.9 copy-start.7
  239.0 1.9 copy-start.8
  239.0 2.0 copy-start.9
  239.0 2.1 copy-start.10
  245.1 21.4 %all-to-all-start = ((bf16[4,160,1024]{2,1,0:T(8,128)(2,1)}), bf16[4,160,1024]{2,1,0:T(8,128)(2,1)}, u32[]{:S(2)}, u32[]{:S(2)}) async-start(bf16[4,160,1024]{2,1,0:T(8,128)(2,1)} %fusion), calls=%async_computation | async-start | bytes 2621440 | tf_op jit(solution)/shard_map/all_to_all | solution.py:257
  249.5 3.1 %copy-start.14 = (f32[3,128]{1,0:T(4,128)S(1)}, f32[3,128]{1,0:T(4,128)}, u32[]{:S(2)}) copy-start(f32[3,128]{1,0:T(4,128)} %get-tuple-element.36) | copy-start | bytes 4612
  249.5 3.2 %copy-start.13 = (f32[3,128]{1,0:T(4,128)S(1)}, f32[3,128]{1,0:T(4,128)}, u32[]{:S(2)}) copy-start(f32[3,128]{1,0:T(4,128)} %get-tuple-element.35) | copy-start | bytes 4612
  249.5 3.3 %copy-start.12 = (f32[3,128]{1,0:T(4,128)S(1)}, f32[3,128]{1,0:T(4,128)}, u32[]{:S(2)}) copy-start(f32[3,128]{1,0:T(4,128)} %get-tuple-element.34) | copy-start | bytes 4612
  249.5 3.4 %copy-start.11 = (f32[3,128]{1,0:T(4,128)S(1)}, f32[3,128]{1,0:T(4,128)}, u32[]{:S(2)}) copy-start(f32[3,128]{1,0:T(4,128)} %get-tuple-element.33) | copy-start | bytes 4612
  251.1 26.3 %copy-start.2 = (bf16[4,128,1024]{2,1,0:T(8,128)(2,1)S(1)}, bf16[4,128,1024]{2,1,0:T(8,128)(2,1)}, u32[]{:S(2)}) copy-start(bf16[4,128,1024]{2,1,0:T(8,128)(2,1)} %get-tuple-element.41) | copy-start | bytes 3145732
  251.1 26.3 %collective-permute-start.2 = (bf16[4,128,1024]{2,1,0:T(8,128)(2,1)}, bf16[4,128,1024]{2,1,0:T(8,128)(2,1)S(1)}, u32[]{:S(2)}, u32[]{:S(2)}) collective-permute-start(bf16[4,128,1024]{2,1,0:T(8,128)(2,1)} %get-tuple-element.42), channel_id=1, source_target_pairs={{0,1},{1,0},{2,3},{3,2},{4,5},{5,4},{6,7},{7,6},{8,9},{9,8},{10,11... | collective-permute-start | bytes 3145736 | tf_op jit(solution)/shard_map/ppermute | solution.py:179
  253.1 1.2 collective-permute-start.5
  269.5 9.5 %collective-permute-start.4 = (f32[32,1024]{1,0:T(8,128)}, f32[32,1024]{1,0:T(8,128)}, u32[]{:S(2)}, u32[]{:S(2)}) collective-permute-start(f32[32,1024]{1,0:T(8,128)} %slice.194), channel_id=1, source_target_pairs={{0,0},{1,4},{2,8},{3,12},{4,16},{5,20},{6,24},{7,28},{8,1},{9,5},{... | collective-permute-start | bytes 393224 | tf_op jit(solution)/shard_map/ppermute | solution.py:260
  271.7 13.8 %all-to-all-start.1 = ((bf16[4,32,1024]{2,1,0:T(8,128)(2,1)}), bf16[4,32,1024]{2,1,0:T(8,128)(2,1)S(1)}, u32[]{:S(2)}, u32[]{:S(2)}) async-start(bf16[4,32,1024]{2,1,0:T(8,128)(2,1)} %bitcast.46), calls=%async_computation.1 | async-start | bytes 524288 | tf_op jit(solution)/shard_map/all_to_all | solution.py:262
  277.4 9.7 %copy-start.1 = (bf16[512,1024]{1,0:T(8,128)(2,1)S(1)}, bf16[512,1024]{1,0:T(8,128)(2,1)}, u32[]{:S(2)}) copy-start(bf16[512,1024]{1,0:T(8,128)(2,1)} %param.13) | copy-start | bytes 3145732
Sparse Core Ops, SparseCore 0:
  15.6 48.5 all-gather.8
  65.7 44.6 all-gather.10
  112.0 44.5 all-gather.12
  158.0 44.6 all-gather.14

commit v3 on v2

v3 whole, which is shorter than its diff:
```python
import functools

import jax
import jax.numpy as jnp
from jax import lax
from jax.experimental import pallas as pl
from jax.experimental.pallas import tpu as pltpu
from jax.sharding import PartitionSpec as P

STEPS = 3
F32 = jnp.float32
BF16 = jnp.bfloat16
NN = (((1,), (0,)), ((), ()))
NT = (((1,), (1,)), ((), ()))
TN = (((0,), (0,)), ((), ()))


def dot(a, b, dims=NN):
    return lax.dot_general(a, b, dims, preferred_element_type=F32)


def forward_kernel(
    chips,
    chip_ref,
    rows_ref,
    rows_t_ref,
    cols_ref,
    rows_own_ref,
    cols_own_ref,
    back_mine_ref,
    back_other_ref,
    emit_l_ref,
    emit_k_ref,
    emit_l_own_ref,
    emit_k_own_ref,
    sum_l_ref,
    sum_k_ref,
    final_ref,
    counts_r_ref,
    counts_c_ref,
    norm_ref,
    held,
    ping,
    pong,
    mixed,
    mixed_own,
    weight,
    pulled,
    send_sem,
    recv_sem,
):
    seqs, rows_chip, _ = chip_ref.shape
    width = rows_ref.shape[0]
    cells = width * cols_ref.shape[1]
    half = back_mine_ref.shape[-1]
    tile = 256
    tiles = width // tile
    hops = chips - 1
    me = lax.axis_index("state")
    core = lax.rem(me, 2)
    chip = me // 2
    right = lax.rem(chip + 1, chips) * 2 + core
    left = lax.rem(chip + chips - 1, chips) * 2 + core

    def rows_of(owner):
        return pl.ds(pl.multiple_of(owner * rows_chip, rows_chip), rows_chip)

    def hop(s, h):
        rows = rows_of(lax.rem(chip + chips - h, chips))
        return pltpu.make_async_remote_copy(
            src_ref=chip_ref.at[s] if h == 0 else held.at[s, rows],
            dst_ref=held.at[s, rows],
            send_sem=send_sem.at[s, h],
            recv_sem=recv_sem.at[s, h],
            device_id={"state": right},
            device_id_type=pl.DeviceIdType.MESH,
        )

    def advance(s, h):
        hop(s, h).wait_recv()
        if h + 1 < hops:
            hop(s, h + 1).start()

    barrier = pltpu.get_barrier_semaphore()
    for neighbour in (left, right):
        pl.semaphore_signal(
            barrier, inc=1, device_id={"state": neighbour}, device_id_type=pl.DeviceIdType.MESH
        )
    pl.semaphore_wait(barrier, 2)
    hop(0, 0).start()
    for s in range(seqs):
        held[s, rows_of(chip), :] = chip_ref[s]
    counts_r_ref[...] = jnp.zeros_like(counts_r_ref)
    counts_c_ref[...] = jnp.zeros_like(counts_c_ref)
    for h in range(hops):
        if h == hops - 1 and seqs > 1:
            hop(1, 0).start()
        advance(0, h)

    def sequence(s, carry):
        @pl.when(s + 2 < seqs)
        def _():
            hop(s + 2, 0).start()

        def follow(step):
            @pl.when(s + 1 < seqs)
            def _():
                for h in range(step * hops // STEPS, (step + 1) * hops // STEPS):
                    advance(s + 1, h)

        messages = (held.at[s], ping, pong)
        for step in range(STEPS):
            alpha = messages[step]
            last = step == STEPS - 1
            v_row = sum_k_ref[s, step : step + 1, :]

            def mix(i, total, alpha=alpha, last=last, step=step, v_row=v_row):
                at = pl.ds(pl.multiple_of(i * tile, tile), tile)
                block = alpha[at, :]
                mixed_own[at, :] = dot(block, cols_own_ref[...]).astype(BF16)
                if not last:
                    mixed[at, :] = dot(block, cols_ref[...]).astype(BF16)
                part = jnp.sum(block.astype(F32) * v_row, axis=1, keepdims=True)
                gain = sum_l_ref[s, at, step : step + 1]
                return total + jnp.sum(part * gain, axis=0, keepdims=True)

            total = lax.fori_loop(0, tiles, mix, jnp.zeros((1, 1), F32))
            norm = total / cells
            inv = 1.0 / norm
            norm_ref[s, step : step + 1, :] = jnp.broadcast_to(norm, (1, norm_ref.shape[2]))
            scaled_k = emit_k_own_ref[s, step : step + 1, :] * inv
            row_k = emit_k_ref[s, step : step + 1, :] * inv

            def weigh(i, carry, step=step, scaled_k=scaled_k):
                at = pl.ds(pl.multiple_of(i * tile, tile), tile)
                gain = emit_l_ref[s, at, step : step + 1]
                weight[at, :half] = (
                    back_mine_ref[step, s, at, :].astype(F32) * (gain * scaled_k[:, :half])
                ).astype(BF16)
                weight[at, half:] = (
                    back_other_ref[step, s, at, :].astype(F32) * (gain * scaled_k[:, half:])
                ).astype(BF16)
                return carry

            lax.fori_loop(0, tiles, weigh, 0)

            if not last:
                fresh = messages[step + 1]

                def move(i, carry, fresh=fresh, row_k=row_k, step=step):
                    at = pl.ds(pl.multiple_of(i * tile, tile), tile)
                    moved = dot(rows_t_ref[at, :], mixed[...])
                    gain = emit_l_ref[s, at, step : step + 1]
                    fresh[at, :] = (moved * (gain * row_k)).astype(BF16)
                    return carry

                lax.fori_loop(0, tiles, move, 0)
            else:
                rows_q = dot(rows_own_ref[...], alpha[...]).astype(BF16)
                moved = dot(rows_q, cols_ref[...])
                gain = emit_l_own_ref[s, :, step : step + 1]
                final_ref[s] = (moved * (gain * row_k)).astype(BF16)

            if not last:
                follow(step)

            def count(i, carry):
                at = pl.ds(pl.multiple_of(i * tile, tile), tile)
                pulled[at, :] = dot(rows_ref[at, :], weight[...]).astype(BF16)
                counts_r_ref[at, :] += dot(weight[at, :], mixed_own[...], NT)
                return carry

            lax.fori_loop(0, tiles, count, 0)
            counts_c_ref[...] += dot(pulled[...], alpha[...], TN)

            if last:
                follow(step)

        return carry

    lax.fori_loop(0, seqs, sequence, 0)
    for s in range(seqs):
        for h in range(hops):
            hop(s, h).wait_send()


def run_forward(chips, *operands):
    chip_rows, rows, _, cols, rows_own, cols_own = operands[:6]
    seqs = chip_rows.shape[0]
    width, cols_all = rows.shape[0], cols.shape[1]
    own_rows, own_cols = rows_own.shape[0], cols_own.shape[1]
    vmem = pl.BlockSpec(memory_space=pltpu.VMEM)
    flops = 2 * seqs * width * cols_all * (4 * width + 3 * 4 * own_cols + 2 * own_rows)
    message = pltpu.VMEM((width, cols_all), BF16)
    narrow = pltpu.VMEM((width, own_cols), BF16)
    return pl.pallas_call(
        functools.partial(forward_kernel, chips),
        out_shape=[
            jax.ShapeDtypeStruct((seqs, own_rows, cols_all), BF16),
            jax.ShapeDtypeStruct((width, width), F32),
            jax.ShapeDtypeStruct((own_cols, cols_all), F32),
            jax.ShapeDtypeStruct((seqs, STEPS, 128), F32),
        ],
        in_specs=[vmem] * len(operands),
        out_specs=[vmem] * 4,
        scratch_shapes=[
            pltpu.VMEM((seqs, width, cols_all), BF16),
            message,
            message,
            message,
            narrow,
            narrow,
            narrow,
            pltpu.SemaphoreType.DMA((seqs, chips - 1)),
            pltpu.SemaphoreType.DMA((seqs, chips - 1)),
        ],
        compiler_params=pltpu.CompilerParams(
            collective_id=0, has_side_effects=True, vmem_limit_bytes=58 * 1024 * 1024
        ),
        cost_estimate=pl.CostEstimate(
            flops=flops, bytes_accessed=40 * 1024 * 1024, transcendentals=0
        ),
    )(*operands)


def on_device(alpha_init, tokens, trans_rows, trans_cols, emit_rows, emit_cols, backward):
    groups = lax.axis_size("state")
    dp = lax.axis_size("dp")
    me = lax.axis_index("state")
    core = me % 2
    seq_dev, rows_dev, width_cols = alpha_init.shape
    width_rows = trans_rows.shape[0]
    cols_dev = width_cols // groups
    half = seq_dev // 2
    pairs = [(d, d ^ 1) for d in range(groups)]
    lines = [list(range(c, groups, 2)) for c in range(2)]

    def swap(x):
        return lax.ppermute(x, "state", pairs)

    def split(x, axis):
        mine = lax.dynamic_slice_in_dim(x, core * half, half, axis)
        return mine, lax.dynamic_slice_in_dim(x, (1 - core) * half, half, axis)

    alpha_mine, alpha_send = split(alpha_init, 0)
    alpha_other = swap(alpha_send)
    chip_rows = jnp.where(
        core == 0,
        jnp.concatenate([alpha_mine, alpha_other], 1),
        jnp.concatenate([alpha_other, alpha_mine], 1),
    )
    back_mine, back_send = split(backward, 1)
    back_other = swap(back_send)

    def own(x, size, axis):
        return jnp.concatenate(
            [
                lax.dynamic_slice_in_dim(x, me * size, size, axis),
                lax.dynamic_slice_in_dim(x, (me + 1 - 2 * core) * size, size, axis),
            ],
            axis,
        )

    rows_t = trans_rows.T
    shared = (trans_rows, rows_t, trans_cols, own(rows_t, rows_dev, 0), own(trans_cols, cols_dev, 1))
    tok = lax.dynamic_slice_in_dim(tokens, core * half, half, 0)
    first = jnp.take(emit_rows, tok, axis=0)
    second = jnp.take(emit_cols, tok, axis=0)
    sum_l = jnp.einsum("stl,il->sit", first, trans_rows, preferred_element_type=F32)
    sum_k = jnp.einsum("stk,jk->stj", second, trans_cols, preferred_element_type=F32)
    emit_l = jnp.swapaxes(first, 1, 2).astype(F32)
    emit_k = second.astype(F32)
    emit_l_own = own(emit_l, rows_dev, 1)
    emit_k_own = own(emit_k, cols_dev, 2)

    final, terms_r, terms_c, norms = run_forward(
        groups // 2,
        chip_rows,
        *shared,
        back_mine,
        back_other,
        emit_l,
        emit_k,
        emit_l_own,
        emit_k_own,
        sum_l,
        sum_k,
    )
    final_mine, final_other = final[:, :rows_dev], swap(final[:, rows_dev:])
    alpha_final = jnp.where(
        core == 0,
        jnp.concatenate([final_mine, final_other], 0),
        jnp.concatenate([final_other, final_mine], 0),
    )
    logs = jnp.sum(jnp.log(norms[:, :, 0]), axis=1)
    logs_other = swap(logs)
    loglik = jnp.where(
        core == 0, jnp.concatenate([logs, logs_other]), jnp.concatenate([logs_other, logs])
    )

    factor = 1.0 / (seq_dev * dp * STEPS)
    chips = groups // 2
    block = width_rows // (groups * dp)
    col_block = width_cols // (groups * dp)
    place = lax.axis_index("dp") * groups + me
    by_core = terms_r.reshape(dp, chips, 2, block, width_rows)

    def of_core(c, cols):
        rows = lax.dynamic_index_in_dim(by_core, c, 2, keepdims=False)
        return jnp.concatenate(
            [rows.reshape(dp, chips * block, width_rows), cols.reshape(dp, col_block, width_cols)], 1
        )

    here = of_core(core, terms_c[:cols_dev])
    there = swap(of_core(1 - core, terms_c[cols_dev:]).astype(BF16))
    both = (here + there.astype(F32)).astype(BF16)
    parts = lax.all_to_all(both, "dp", 0, 0, tiled=True)
    sums = jnp.sum(parts.astype(F32), axis=0)
    order = [(d * groups + g, g * dp + d) for d in range(dp) for g in range(groups)]
    sums_c = lax.ppermute(sums[chips * block :], ("dp", "state"), order)
    line = sums[: chips * block].reshape(chips, block, width_rows).astype(BF16)
    line = lax.all_to_all(line, "state", 0, 0, tiled=True, axis_index_groups=lines)
    sums_r = jnp.sum(line.astype(F32), axis=0)
    counts_rows = (
        lax.dynamic_slice_in_dim(rows_t, place * block, block, 0).astype(F32) * sums_r * factor
    ).T
    counts_cols = (
        lax.dynamic_slice_in_dim(trans_cols, place * col_block, col_block, 1).astype(F32)
        * sums_c.T
        * factor
    )
    return (alpha_final, counts_rows, counts_cols, loglik)


def solution(mesh):
    return jax.shard_map(
        on_device,
        mesh=mesh,
        in_specs=(
            P("dp", "state", None),
            P("dp", None),
            P(),
            P(),
            P(),
            P(),
            P(None, "dp", None, "state"),
        ),
        out_specs=(
            P("dp", "state", None),
            P(None, ("dp", "state")),
            P(None, ("dp", "state")),
            P("dp"),
        ),
        check_vma=False,
    )
```

time: 294 us -> 269 us (0.915)
  waiting for transfers between devices: 89.9 us -> 15.3 us
  Pallas kernels: 126 us -> 184 us
  between operations: 14.1 us -> 0.81 us
  other arithmetic: 16 us -> 21.1 us
    all_gather x4 -> x0, waiting for transfers between devices: 68.4 us -> none  [on_device(): lax.all_gather(chip_rows[s], 'state', axis=0, tiled=True, axis_index_grou...]
    pallas_call x4 -> x1, Pallas kernels: 126 us -> 184 us  [run_forward(): pl.pallas_call(functools.partial(forward_kernel, chips), out_shape=[jax.S...]
    concatenate x2 -> x4, other arithmetic: 1.78 us -> 6.41 us  [own(): jnp.concatenate([lax.dynamic_slice_in_dim(x, me * size, size, axis), lax....]
    dynamic_slice x4, local copies, waits for them, and re-layouts: 0.24 us -> 4.51 us  [own(): lax.dynamic_slice_in_dim(x, me * size, size, axis)]
  transfers between devices with their start and end apart: 12 -> 8, of which waited for: 9 -> 4; matrix products, arithmetic and copies ran while one was open for 12% -> 16% of each run, Pallas kernels for 32% -> 0%
where the time goes in v3:
time: 269 us; the launch traced here: 268 us
  Pallas kernels  184 us (68%)
  local copies, waits for them, and re-layouts  30.5 us (11%)
  other arithmetic  21.1 us (8%)
  waiting for transfers between devices  15.3 us (6%)
  starting transfers between devices  12.6 us (5%)
  matrix products  3.89 us (1%)
    pallas_call x1, Pallas kernels, run_forward(): pl.pallas_call(functools.partial(forward_kernel, chips), out_shape=[jax.S...  184 us
    all_to_all x1, waiting for transfers between devices, on_device(): parts = lax.all_to_all(both, 'dp', 0, 0, tiled=True)  9.02 us
    all_to_all x1, starting transfers between devices, on_device(): lax.all_to_all(line, 'state', 0, 0, tiled=True, axis_index_groups=lines)  7.2 us
    concatenate x4, other arithmetic, own(): jnp.concatenate([lax.dynamic_slice_in_dim(x, me * size, size, axis), lax....  6.41 us
    dynamic_slice x1, local copies, waits for them, and re-layouts, split(): return (mine, lax.dynamic_slice_in_dim(x, (1 - core) * half, half, axis))  6.23 us
  transfers between devices with their start and end apart: 8, of which 4 were waited for; matrix products, arithmetic and copies ran while one was open for 16% of the time, Pallas kernels for 0%

profile of v3, /device:TPU:0, one launch (start us, length us, event | category | flops | bytes accessed | tf_op | source)
XLA Modules:
  0.0 267.8 jit_solution(11243185542114532845)
XLA Ops:
  0.6 0.0 copy-start
  0.7 0.0 copy-start.2
  0.7 6.2 %constant_dynamic-slice_fusion.5 = (bf16[3,4,1024,128]{3,2,1,0:T(8,128)(2,1)}, bf16[3,4,1024,128]{3,2,1,0:T(8,128)(2,1)}) fusion(bf16[3,8,1024,128]{3,2,1,0:T(8,128)(2,1)} %param.15, s32[]{:T(128)S(6)} %select_n.74, s32[]{:T(128)S(6)} %select_n.73), kind=kLoop, calls=%fused_computation.43 | loop fusion | bytes 12582920 | tf_op jit(solution)/shard_map/dynamic_slice | solution.py:243
  6.9 0.5 collective-permute-start.1
  7.4 0.0 copy-done.2
  7.4 1.2 constant_dynamic-slice_fusion.10
  8.6 0.1 collective-permute-start
  8.6 0.0 copy-done.7
  8.6 0.1 compare_and_fusion
  8.7 0.1 copy.59
  8.8 0.1 reshape.60
  8.9 0.0 copy-done
  8.9 0.6 gather_fusion
  9.5 0.5 copy.60
  10.0 0.1 copy.58
  10.1 3.9 %copy.55 = bf16[1024,1024]{0,1:T(8,128)(2,1)} copy(bf16[1024,1024]{1,0:T(8,128)(2,1)} %rows_ref.1) | data formatting | bytes 4194304 | tf_op args[2]
  14.1 2.0 gather_fusion.1
  16.1 0.1 fusion.13.emit_k_ref
  16.2 0.0 copy-start.5
  16.2 1.6 fusion.8
  17.8 0.0 copy-done.5
  17.8 0.8 dynamic-slice_bitcast_fusion.1
  18.7 1.9 dynamic-slice_bitcast_fusion.3
  20.6 1.8 constant_dynamic-slice_fusion.8
  22.3 0.6 pad_maximum_fusion.4.emit_k_own_ref
  22.9 2.0 pad_maximum_fusion.3.emit_l_own_ref
  25.0 2.0 pad_maximum_fusion.1.rows_own_ref
  27.0 1.8 pad_maximum_fusion.2.cols_own_ref
  28.8 0.0 copy-done.1
  28.8 1.3 fusion.1.sum_k_ref
  30.1 2.6 fusion.5.sum_l_ref
  32.7 0.0 collective-permute-done
  32.7 3.9 %maximum_select_fusion.chip_ref = bf16[4,256,1024]{2,1,0:T(8,128)(2,1)} fusion(bf16[4,128,1024]{2,1,0:T(8,128)(2,1)} %collective-permute-done, bf16[4,128,1024]{2,1,0:T(8,128)(2,1)S(1)} %get-tuple-element.25, pred[]{:T(512)S(6)} %eq.4), kind=kLoop, calls=%fused_computation.5 | loop fusion | flops 9437184 | bytes 4194305 | tf_op jit(solution)/shard_map/jit(_where)/select_n | solution.py:247
  36.5 0.0 collective-permute-done.1.back_other_ref
  36.5 183.6 %shard_map.102 = (bf16[4,256,1024]{2,1,0:T(8,128)(2,1)}, f32[1024,1024]{1,0:T(8,128)}, f32[256,1024]{1,0:T(8,128)}, f32[4,3,128]{2,1,0:T(4,128)}) custom-call(bf16[4,256,1024]{2,1,0:T(8,128)(2,1)} %maximum_select_fusion.chip_ref, bf16[1024,1024]{1,0:T(8,128)(2,1)} %rows_ref.1, bf16[1024,1024]{1,0:T(8,128)(2,1)} %bitcast.37, bf16[1024,1024]{1,0:T(8,128)(2,1)} %cols_ref.1, ...), custom_call_target="tpu_custom_call" | custom-call | flops 64424509440 | bytes 41943040 | tf_op jit(solution)/shard_map/pallas_call | solution.py:196
  220.1 1.1 slice.41
  221.2 1.8 dynamic-slice_convert_fusion
  223.1 1.2 pad_maximum_fusion
  224.2 0.0 collective-permute-start.3
  224.2 0.0 copy-done.4
  224.3 1.7 constant_dynamic-slice_fusion.1
  226.0 1.4 collective-permute-done.3
  227.5 1.5 fusion
  229.0 3.7 %all-to-all-start = ((bf16[4,160,1024]{2,1,0:T(8,128)(2,1)}), bf16[4,160,1024]{2,1,0:T(8,128)(2,1)S(1)}, u32[]{:S(2)}, u32[]{:S(2)}) async-start(bf16[4,160,1024]{2,1,0:T(8,128)(2,1)} %fusion), calls=%async_computation | async-start | bytes 2621440 | tf_op jit(solution)/shard_map/all_to_all | solution.py:317
  232.7 2.8 %fusion.17 = (bf16[4,128,1024]{2,1,0:T(8,128)(2,1)S(1)}, bf16[4,128,1024]{2,1,0:T(8,128)(2,1)}) fusion(bf16[4,256,1024]{2,1,0:T(8,128)(2,1)} %get-tuple-element.9), kind=kLoop, calls=%fused_computation.54 | loop fusion | bytes 4194304 | tf_op jit(solution)/shard_map/slice | solution.py:289
  235.5 0.0 collective-permute-start.2
  235.5 1.8 constant_dynamic-slice_fusion
  237.3 1.1 copy.73
  238.4 0.0 copy-done.6
  238.4 0.1 log_reduce_fusion
  238.5 0.6 collective-permute-start.5
  239.1 0.8 collective-permute-done.5
  239.9 0.6 broadcast_select_fusion.4
  240.5 9.0 %all-to-all-done = bf16[4,160,1024]{2,1,0:T(8,128)(2,1)S(1)} async-done(((bf16[4,160,1024]{2,1,0:T(8,128)(2,1)}), bf16[4,160,1024]{2,1,0:T(8,128)(2,1)S(1)}, u32[]{:S(2)}, u32[]{:S(2)}) %all-to-all-start) | async-done | bytes 1310752 | tf_op jit(solution)/shard_map/all_to_all | solution.py:317
  249.5 0.2 convert_reduce_fusion
  249.8 0.8 slice.40
  250.5 0.7 collective-permute-start.4
  251.2 7.2 %all-to-all-start.1 = ((bf16[4,32,1024]{2,1,0:T(8,128)(2,1)}), bf16[4,32,1024]{2,1,0:T(8,128)(2,1)S(1)}, u32[]{:S(2)}, u32[]{:S(2)}) async-start(bf16[4,32,1024]{2,1,0:T(8,128)(2,1)} %bitcast.14), calls=%async_computation.1 | async-start | bytes 524288 | tf_op jit(solution)/shard_map/all_to_all | solution.py:322
  258.4 0.0 collective-permute-done.2
  258.4 3.2 %maximum_select_fusion.1 = bf16[8,128,1024]{2,1,0:T(8,128)(2,1)} fusion(bf16[4,128,1024]{2,1,0:T(8,128)(2,1)} %collective-permute-done.2, bf16[4,128,1024]{2,1,0:T(8,128)(2,1)S(1)} %get-tuple-element.17, pred[]{:T(512)S(6)} %eq.4), kind=kLoop, calls=%fused_computation.6 | loop fusion | flops 3145728 | bytes 4194305 | tf_op jit(solution)/shard_map/jit(_where)/select_n | solution.py:290
  261.6 0.0 collective-permute-done.4
  261.6 0.7 fusion.11
  262.3 4.0 %all-to-all-done.1 = bf16[4,32,1024]{2,1,0:T(8,128)(2,1)S(1)} async-done(((bf16[4,32,1024]{2,1,0:T(8,128)(2,1)}), bf16[4,32,1024]{2,1,0:T(8,128)(2,1)S(1)}, u32[]{:S(2)}, u32[]{:S(2)}) %all-to-all-start.1) | async-done | bytes 262176 | tf_op jit(solution)/shard_map/all_to_all | solution.py:322
  266.3 1.5 fusion.12
  (13 shorter events, 0.2 us)
Async XLA Ops:
  0.6 8.3 %copy-start = (bf16[512,1024]{1,0:T(8,128)(2,1)S(1)}, bf16[512,1024]{1,0:T(8,128)(2,1)}, u32[]{:S(2)}) copy-start(bf16[512,1024]{1,0:T(8,128)(2,1)} %param.13) | copy-start | bytes 3145732
  0.7 6.7 %copy-start.2 = (bf16[8,128,1024]{2,1,0:T(8,128)(2,1)S(1)}, bf16[8,128,1024]{2,1,0:T(8,128)(2,1)}, u32[]{:S(2)}) copy-start(bf16[8,128,1024]{2,1,0:T(8,128)(2,1)} %param.9) | copy-start | bytes 6291460
  6.9 1.7 copy-start.7
  6.9 29.6 %collective-permute-start.1 = (bf16[3,4,1024,128]{3,2,1,0:T(8,128)(2,1)}, bf16[3,4,1024,128]{3,2,1,0:T(8,128)(2,1)}, u32[]{:S(2)}, u32[]{:S(2)}) collective-permute-start(bf16[3,4,1024,128]{3,2,1,0:T(8,128)(2,1)} %get-tuple-element.15), channel_id=1, source_target_pairs={{0,1},{1,0},{2,3},{3,2},{4,5},{5,4},{6,7},{7,6},{8,9},{9,8},{10,11... | collective-permute-start | bytes 9437192 | tf_op jit(solution)/shard_map/ppermute | solution.py:239
  8.6 24.1 %collective-permute-start = (bf16[4,128,1024]{2,1,0:T(8,128)(2,1)}, bf16[4,128,1024]{2,1,0:T(8,128)(2,1)}, u32[]{:S(2)}, u32[]{:S(2)}) collective-permute-start(bf16[4,128,1024]{2,1,0:T(8,128)(2,1)} %get-tuple-element.26), channel_id=1, source_target_pairs={{0,1},{1,0},{2,3},{3,2},{4,5},{5,4},{6,7},{7,6},{8,9},{9,8},{10,11... | collective-permute-start | bytes 3145736 | tf_op jit(solution)/shard_map/ppermute | solution.py:239
  16.2 1.7 copy-start.5
  22.9 5.8 %copy-start.1 = (bf16[1024,1024]{1,0:T(8,128)(2,1)S(1)}, bf16[1024,1024]{1,0:T(8,128)(2,1)}, u32[]{:S(2)}) copy-start(bf16[1024,1024]{1,0:T(8,128)(2,1)} %cols_ref.1) | copy-start | bytes 6291460
  25.0 5.1 %copy-start.3 = (bf16[1024,1024]{1,0:T(8,128)(2,1)S(1)}, bf16[1024,1024]{1,0:T(8,128)(2,1)}, u32[]{:S(2)}) copy-start(bf16[1024,1024]{1,0:T(8,128)(2,1)} %rows_ref.1) | copy-start | bytes 6291460
  221.2 3.0 %copy-start.4 = (f32[256,1024]{1,0:T(8,128)S(1)}, f32[256,1024]{1,0:T(8,128)}, u32[]{:S(2)}) copy-start(f32[256,1024]{1,0:T(8,128)} %get-tuple-element.11) | copy-start | bytes 3145732
  224.2 3.2 %collective-permute-start.3 = (bf16[4,160,1024]{2,1,0:T(8,128)(2,1)}, bf16[4,160,1024]{2,1,0:T(8,128)(2,1)S(1)}, u32[]{:S(2)}, u32[]{:S(2)}) collective-permute-start(bf16[4,160,1024]{2,1,0:T(8,128)(2,1)} %pad_maximum_fusion), channel_id=1, source_target_pairs={{0,1},{1,0},{2,3},{3,2},{4,5},{5,4},{6,7},{7,6},{8,9},{9,8},{10,11... | collective-permute-start | bytes 3932168 | tf_op jit(solution)/shard_map/ppermute | solution.py:239
  229.0 20.5 %all-to-all-start = ((bf16[4,160,1024]{2,1,0:T(8,128)(2,1)}), bf16[4,160,1024]{2,1,0:T(8,128)(2,1)S(1)}, u32[]{:S(2)}, u32[]{:S(2)}) async-start(bf16[4,160,1024]{2,1,0:T(8,128)(2,1)} %fusion), calls=%async_computation | async-start | bytes 2621440 | tf_op jit(solution)/shard_map/all_to_all | solution.py:317
  232.7 5.7 %copy-start.6 = (f32[4,3,128]{2,1,0:T(4,128)S(1)}, f32[4,3,128]{2,1,0:T(4,128)}, u32[]{:S(2)}) copy-start(f32[4,3,128]{2,1,0:T(4,128)} %get-tuple-element.12) | copy-start | bytes 18436
  235.5 22.9 %collective-permute-start.2 = (bf16[4,128,1024]{2,1,0:T(8,128)(2,1)}, bf16[4,128,1024]{2,1,0:T(8,128)(2,1)}, u32[]{:S(2)}, u32[]{:S(2)}) collective-permute-start(bf16[4,128,1024]{2,1,0:T(8,128)(2,1)} %get-tuple-element.18), channel_id=1, source_target_pairs={{0,1},{1,0},{2,3},{3,2},{4,5},{5,4},{6,7},{7,6},{8,9},{9,8},{10,11... | collective-permute-start | bytes 3145736 | tf_op jit(solution)/shard_map/ppermute | solution.py:239
  238.5 1.4 collective-permute-start.5
  250.5 11.1 %collective-permute-start.4 = (f32[32,1024]{1,0:T(8,128)S(1)}, f32[32,1024]{1,0:T(8,128)S(1)}, u32[]{:S(2)}, u32[]{:S(2)}) collective-permute-start(f32[32,1024]{1,0:T(8,128)S(1)} %slice.36), channel_id=1, source_target_pairs={{0,0},{1,4},{2,8},{3,12},{4,16},{5,20},{6,24},{7,28},{8,1},{9,5},{... | collective-permute-start | bytes 393224 | tf_op jit(solution)/shard_map/ppermute | solution.py:320
  251.2 15.1 %all-to-all-start.1 = ((bf16[4,32,1024]{2,1,0:T(8,128)(2,1)}), bf16[4,32,1024]{2,1,0:T(8,128)(2,1)S(1)}, u32[]{:S(2)}, u32[]{:S(2)}) async-start(bf16[4,32,1024]{2,1,0:T(8,128)(2,1)} %bitcast.14), calls=%async_computation.1 | async-start | bytes 524288 | tf_op jit(solution)/shard_map/all_to_all | solution.py:322

commit v4 on v3

--- a/solution.py
+++ b/solution.py
@@ -53,7 +53,7 @@
     width = rows_ref.shape[0]
     cells = width * cols_ref.shape[1]
     half = back_mine_ref.shape[-1]
-    tile = 256
+    tile = 512
     tiles = width // tile
     hops = chips - 1
     me = lax.axis_index("state")

time: 269 us -> 265 us (0.985)
  Pallas kernels: 184 us -> 180 us
    pallas_call x1, Pallas kernels: 184 us -> 180 us  [run_forward(): pl.pallas_call(functools.partial(forward_kernel, chips), out_shape=[jax.S...]
where the time goes in v4:
time: 265 us; the launch traced here: 264 us
  Pallas kernels  180 us (68%)
  local copies, waits for them, and re-layouts  30.5 us (12%)
  other arithmetic  21.1 us (8%)
  waiting for transfers between devices  15.3 us (6%)
  starting transfers between devices  12.6 us (5%)
  matrix products  3.89 us (1%)
    pallas_call x1, Pallas kernels, run_forward(): pl.pallas_call(functools.partial(forward_kernel, chips), out_shape=[jax.S...  180 us
    all_to_all x1, waiting for transfers between devices, on_device(): parts = lax.all_to_all(both, 'dp', 0, 0, tiled=True)  9.02 us
    all_to_all x1, starting transfers between devices, on_device(): lax.all_to_all(line, 'state', 0, 0, tiled=True, axis_index_groups=lines)  7.2 us
    concatenate x4, other arithmetic, own(): jnp.concatenate([lax.dynamic_slice_in_dim(x, me * size, size, axis), lax....  6.41 us
    dynamic_slice x1, local copies, waits for them, and re-layouts, split(): return (mine, lax.dynamic_slice_in_dim(x, (1 - core) * half, half, axis))  6.23 us
  transfers between devices with their start and end apart: 8, of which 4 were waited for; matrix products, arithmetic and copies ran while one was open for 16% of the time, Pallas kernels for 0%

profile of v4, /device:TPU:0, one launch (start us, length us, event | category | flops | bytes accessed | tf_op | source)
XLA Modules:
  0.0 264.0 jit_solution(12764099331403517472)
XLA Ops:
  0.6 0.0 copy-start
  0.7 0.0 copy-start.2
  0.7 6.2 %constant_dynamic-slice_fusion.5 = (bf16[3,4,1024,128]{3,2,1,0:T(8,128)(2,1)}, bf16[3,4,1024,128]{3,2,1,0:T(8,128)(2,1)}) fusion(bf16[3,8,1024,128]{3,2,1,0:T(8,128)(2,1)} %param.15, s32[]{:T(128)S(6)} %select_n.74, s32[]{:T(128)S(6)} %select_n.73), kind=kLoop, calls=%fused_computation.43 | loop fusion | bytes 12582920 | tf_op jit(solution)/shard_map/dynamic_slice | solution.py:243
  6.9 0.5 collective-permute-start.1
  7.4 0.0 copy-done.2
  7.4 1.2 constant_dynamic-slice_fusion.10
  8.6 0.1 collective-permute-start
  8.6 0.0 copy-done.7
  8.6 0.1 compare_and_fusion
  8.7 0.1 copy.59
  8.8 0.1 reshape.60
  8.9 0.0 copy-done
  8.9 0.6 gather_fusion
  9.5 0.5 copy.60
  10.0 0.1 copy.58
  10.1 3.9 %copy.55 = bf16[1024,1024]{0,1:T(8,128)(2,1)} copy(bf16[1024,1024]{1,0:T(8,128)(2,1)} %rows_ref.1) | data formatting | bytes 4194304 | tf_op args[2]
  14.1 2.0 gather_fusion.1
  16.1 0.1 fusion.13.emit_k_ref
  16.2 0.0 copy-start.5
  16.2 1.6 fusion.8
  17.8 0.0 copy-done.5
  17.8 0.8 dynamic-slice_bitcast_fusion.1
  18.7 1.9 dynamic-slice_bitcast_fusion.3
  20.6 1.8 constant_dynamic-slice_fusion.8
  22.3 0.6 pad_maximum_fusion.4.emit_k_own_ref
  22.9 2.0 pad_maximum_fusion.3.emit_l_own_ref
  25.0 2.0 pad_maximum_fusion.1.rows_own_ref
  27.0 1.8 pad_maximum_fusion.2.cols_own_ref
  28.8 0.0 copy-done.1
  28.8 1.3 fusion.1.sum_k_ref
  30.1 0.0 copy-done.3
  30.1 2.6 fusion.5.sum_l_ref
  32.7 0.0 collective-permute-done
  32.7 3.9 %maximum_select_fusion.chip_ref = bf16[4,256,1024]{2,1,0:T(8,128)(2,1)} fusion(bf16[4,128,1024]{2,1,0:T(8,128)(2,1)} %collective-permute-done, bf16[4,128,1024]{2,1,0:T(8,128)(2,1)S(1)} %get-tuple-element.25, pred[]{:T(512)S(6)} %eq.4), kind=kLoop, calls=%fused_computation.5 | loop fusion | flops 9437184 | bytes 4194305 | tf_op jit(solution)/shard_map/jit(_where)/select_n | solution.py:247
  36.5 0.0 collective-permute-done.1.back_other_ref
  36.5 179.8 %shard_map.102 = (bf16[4,256,1024]{2,1,0:T(8,128)(2,1)}, f32[1024,1024]{1,0:T(8,128)}, f32[256,1024]{1,0:T(8,128)}, f32[4,3,128]{2,1,0:T(4,128)}) custom-call(bf16[4,256,1024]{2,1,0:T(8,128)(2,1)} %maximum_select_fusion.chip_ref, bf16[1024,1024]{1,0:T(8,128)(2,1)} %rows_ref.1, bf16[1024,1024]{1,0:T(8,128)(2,1)} %bitcast.37, bf16[1024,1024]{1,0:T(8,128)(2,1)} %cols_ref.1, ...), custom_call_target="tpu_custom_call" | custom-call | flops 64424509440 | bytes 41943040 | tf_op jit(solution)/shard_map/pallas_call | solution.py:196
  216.3 1.1 slice.41
  217.4 0.0 copy-start.4
  217.4 1.8 dynamic-slice_convert_fusion
  219.3 1.2 pad_maximum_fusion
  220.4 0.0 collective-permute-start.3
  220.5 1.7 constant_dynamic-slice_fusion.1
  222.2 1.4 collective-permute-done.3
  223.7 1.5 fusion
  225.2 3.7 %all-to-all-start = ((bf16[4,160,1024]{2,1,0:T(8,128)(2,1)}), bf16[4,160,1024]{2,1,0:T(8,128)(2,1)S(1)}, u32[]{:S(2)}, u32[]{:S(2)}) async-start(bf16[4,160,1024]{2,1,0:T(8,128)(2,1)} %fusion), calls=%async_computation | async-start | bytes 2621440 | tf_op jit(solution)/shard_map/all_to_all | solution.py:317
  228.9 2.8 %fusion.17 = (bf16[4,128,1024]{2,1,0:T(8,128)(2,1)S(1)}, bf16[4,128,1024]{2,1,0:T(8,128)(2,1)}) fusion(bf16[4,256,1024]{2,1,0:T(8,128)(2,1)} %get-tuple-element.9), kind=kLoop, calls=%fused_computation.54 | loop fusion | bytes 4194304 | tf_op jit(solution)/shard_map/slice | solution.py:289
  231.7 0.0 collective-permute-start.2
  231.7 1.8 constant_dynamic-slice_fusion
  233.5 1.1 copy.73
  234.6 0.1 log_reduce_fusion
  234.7 0.6 collective-permute-start.5
  235.3 0.8 collective-permute-done.5
  236.1 0.6 broadcast_select_fusion.4
  236.7 9.0 %all-to-all-done = bf16[4,160,1024]{2,1,0:T(8,128)(2,1)S(1)} async-done(((bf16[4,160,1024]{2,1,0:T(8,128)(2,1)}), bf16[4,160,1024]{2,1,0:T(8,128)(2,1)S(1)}, u32[]{:S(2)}, u32[]{:S(2)}) %all-to-all-start) | async-done | bytes 1310752 | tf_op jit(solution)/shard_map/all_to_all | solution.py:317
  245.7 0.2 convert_reduce_fusion
  246.0 0.8 slice.40
  246.7 0.7 collective-permute-start.4
  247.4 7.2 %all-to-all-start.1 = ((bf16[4,32,1024]{2,1,0:T(8,128)(2,1)}), bf16[4,32,1024]{2,1,0:T(8,128)(2,1)S(1)}, u32[]{:S(2)}, u32[]{:S(2)}) async-start(bf16[4,32,1024]{2,1,0:T(8,128)(2,1)} %bitcast.14), calls=%async_computation.1 | async-start | bytes 524288 | tf_op jit(solution)/shard_map/all_to_all | solution.py:322
  254.6 0.0 collective-permute-done.2
  254.6 3.2 %maximum_select_fusion.1 = bf16[8,128,1024]{2,1,0:T(8,128)(2,1)} fusion(bf16[4,128,1024]{2,1,0:T(8,128)(2,1)} %collective-permute-done.2, bf16[4,128,1024]{2,1,0:T(8,128)(2,1)S(1)} %get-tuple-element.17, pred[]{:T(512)S(6)} %eq.4), kind=kLoop, calls=%fused_computation.6 | loop fusion | flops 3145728 | bytes 4194305 | tf_op jit(solution)/shard_map/jit(_where)/select_n | solution.py:290
  257.8 0.0 collective-permute-done.4
  257.8 0.7 fusion.11
  258.5 4.0 %all-to-all-done.1 = bf16[4,32,1024]{2,1,0:T(8,128)(2,1)S(1)} async-done(((bf16[4,32,1024]{2,1,0:T(8,128)(2,1)}), bf16[4,32,1024]{2,1,0:T(8,128)(2,1)S(1)}, u32[]{:S(2)}, u32[]{:S(2)}) %all-to-all-start.1) | async-done | bytes 262176 | tf_op jit(solution)/shard_map/all_to_all | solution.py:322
  262.5 1.5 fusion.12
  (13 shorter events, 0.2 us)
Async XLA Ops:
  0.6 8.3 %copy-start = (bf16[512,1024]{1,0:T(8,128)(2,1)S(1)}, bf16[512,1024]{1,0:T(8,128)(2,1)}, u32[]{:S(2)}) copy-start(bf16[512,1024]{1,0:T(8,128)(2,1)} %param.13) | copy-start | bytes 3145732
  0.7 6.7 %copy-start.2 = (bf16[8,128,1024]{2,1,0:T(8,128)(2,1)S(1)}, bf16[8,128,1024]{2,1,0:T(8,128)(2,1)}, u32[]{:S(2)}) copy-start(bf16[8,128,1024]{2,1,0:T(8,128)(2,1)} %param.9) | copy-start | bytes 6291460
  6.9 1.7 copy-start.7
  6.9 29.6 %collective-permute-start.1 = (bf16[3,4,1024,128]{3,2,1,0:T(8,128)(2,1)}, bf16[3,4,1024,128]{3,2,1,0:T(8,128)(2,1)}, u32[]{:S(2)}, u32[]{:S(2)}) collective-permute-start(bf16[3,4,1024,128]{3,2,1,0:T(8,128)(2,1)} %get-tuple-element.15), channel_id=1, source_target_pairs={{0,1},{1,0},{2,3},{3,2},{4,5},{5,4},{6,7},{7,6},{8,9},{9,8},{10,11... | collective-permute-start | bytes 9437192 | tf_op jit(solution)/shard_map/ppermute | solution.py:239
  8.6 24.1 %collective-permute-start = (bf16[4,128,1024]{2,1,0:T(8,128)(2,1)}, bf16[4,128,1024]{2,1,0:T(8,128)(2,1)}, u32[]{:S(2)}, u32[]{:S(2)}) collective-permute-start(bf16[4,128,1024]{2,1,0:T(8,128)(2,1)} %get-tuple-element.26), channel_id=1, source_target_pairs={{0,1},{1,0},{2,3},{3,2},{4,5},{5,4},{6,7},{7,6},{8,9},{9,8},{10,11... | collective-permute-start | bytes 3145736 | tf_op jit(solution)/shard_map/ppermute | solution.py:239
  16.2 1.7 copy-start.5
  22.9 5.8 %copy-start.1 = (bf16[1024,1024]{1,0:T(8,128)(2,1)S(1)}, bf16[1024,1024]{1,0:T(8,128)(2,1)}, u32[]{:S(2)}) copy-start(bf16[1024,1024]{1,0:T(8,128)(2,1)} %cols_ref.1) | copy-start | bytes 6291460
  25.0 5.1 %copy-start.3 = (bf16[1024,1024]{1,0:T(8,128)(2,1)S(1)}, bf16[1024,1024]{1,0:T(8,128)(2,1)}, u32[]{:S(2)}) copy-start(bf16[1024,1024]{1,0:T(8,128)(2,1)} %rows_ref.1) | copy-start | bytes 6291460
  217.4 3.0 %copy-start.4 = (f32[256,1024]{1,0:T(8,128)S(1)}, f32[256,1024]{1,0:T(8,128)}, u32[]{:S(2)}) copy-start(f32[256,1024]{1,0:T(8,128)} %get-tuple-element.11) | copy-start | bytes 3145732
  220.4 3.2 %collective-permute-start.3 = (bf16[4,160,1024]{2,1,0:T(8,128)(2,1)}, bf16[4,160,1024]{2,1,0:T(8,128)(2,1)S(1)}, u32[]{:S(2)}, u32[]{:S(2)}) collective-permute-start(bf16[4,160,1024]{2,1,0:T(8,128)(2,1)} %pad_maximum_fusion), channel_id=1, source_target_pairs={{0,1},{1,0},{2,3},{3,2},{4,5},{5,4},{6,7},{7,6},{8,9},{9,8},{10,11... | collective-permute-start | bytes 3932168 | tf_op jit(solution)/shard_map/ppermute | solution.py:239
  225.2 20.5 %all-to-all-start = ((bf16[4,160,1024]{2,1,0:T(8,128)(2,1)}), bf16[4,160,1024]{2,1,0:T(8,128)(2,1)S(1)}, u32[]{:S(2)}, u32[]{:S(2)}) async-start(bf16[4,160,1024]{2,1,0:T(8,128)(2,1)} %fusion), calls=%async_computation | async-start | bytes 2621440 | tf_op jit(solution)/shard_map/all_to_all | solution.py:317
  228.9 5.7 %copy-start.6 = (f32[4,3,128]{2,1,0:T(4,128)S(1)}, f32[4,3,128]{2,1,0:T(4,128)}, u32[]{:S(2)}) copy-start(f32[4,3,128]{2,1,0:T(4,128)} %get-tuple-element.12) | copy-start | bytes 18436
  231.7 22.9 %collective-permute-start.2 = (bf16[4,128,1024]{2,1,0:T(8,128)(2,1)}, bf16[4,128,1024]{2,1,0:T(8,128)(2,1)}, u32[]{:S(2)}, u32[]{:S(2)}) collective-permute-start(bf16[4,128,1024]{2,1,0:T(8,128)(2,1)} %get-tuple-element.18), channel_id=1, source_target_pairs={{0,1},{1,0},{2,3},{3,2},{4,5},{5,4},{6,7},{7,6},{8,9},{9,8},{10,11... | collective-permute-start | bytes 3145736 | tf_op jit(solution)/shard_map/ppermute | solution.py:239
  234.7 1.4 collective-permute-start.5
  246.7 11.1 %collective-permute-start.4 = (f32[32,1024]{1,0:T(8,128)S(1)}, f32[32,1024]{1,0:T(8,128)S(1)}, u32[]{:S(2)}, u32[]{:S(2)}) collective-permute-start(f32[32,1024]{1,0:T(8,128)S(1)} %slice.36), channel_id=1, source_target_pairs={{0,0},{1,4},{2,8},{3,12},{4,16},{5,20},{6,24},{7,28},{8,1},{9,5},{... | collective-permute-start | bytes 393224 | tf_op jit(solution)/shard_map/ppermute | solution.py:320
  247.4 15.1 %all-to-all-start.1 = ((bf16[4,32,1024]{2,1,0:T(8,128)(2,1)}), bf16[4,32,1024]{2,1,0:T(8,128)(2,1)S(1)}, u32[]{:S(2)}, u32[]{:S(2)}) async-start(bf16[4,32,1024]{2,1,0:T(8,128)(2,1)} %bitcast.14), calls=%async_computation.1 | async-start | bytes 524288 | tf_op jit(solution)/shard_map/all_to_all | solution.py:322
